TPU v7x, 32 devices: a whole 2x2x4 slice. The times are simulated.
32 devices in a mesh: section: 4 (over y, x), dp: 8 (over z, core).
Axes of the slice: x: 2, y: 2, z: 4, core: 2. Of those that a mesh axis runs over, the one named last changes fastest.
Arguments:
- lidar: bfloat16 [4, 8, 16, 16, 256], P('section', 'dp'), may hold values from -6 to 6
- context: bfloat16 [4, 8, 128, 80], P('section', 'dp'), may hold values from -60 to 60
- depth_logits: bfloat16 [4, 8, 128, 118], P('section', 'dp'), may hold values from -9 to 9
- cell_index: int32 [4, 8, 128, 118], P('section', 'dp'), may hold values from 0 to 255
- unite_weight: bfloat16 [9, 336, 256], replicated, may hold values from -0.109375 to 0.109375
- unite_gain: float32 [256], replicated, may hold values from 0.5 to 1.5
- unite_bias: float32 [256], replicated, may hold values from -3 to 3
- first_weight: bfloat16 [4, 9, 256, 256], P('section'), may hold values from -0.125 to 0.125
- second_weight: bfloat16 [4, 9, 256, 256], P('section'), may hold values from -0.125 to 0.125
- first_gain: float32 [4, 256], P('section'), may hold values from 0.5 to 1.5
- first_bias: float32 [4, 256], P('section'), may hold values from -3 to 3
- second_gain: float32 [4, 256], P('section'), may hold values from 0.5 to 1.5
- second_bias: float32 [4, 256], P('section'), may hold values from -3 to 3
- cotangent: bfloat16 [4, 8, 16, 16, 256], P(None, 'dp'), may hold values from -6 to 6
Outputs:
- activations: float32 [4, 8, 16, 16, 256], P('section', 'dp')
- grad_lidar: float32 [4, 8, 16, 16, 256], P('section', 'dp')
- grad_context: float32 [4, 8, 128, 80], P('section', 'dp')
- grad_depth_logits: float32 [4, 8, 128, 118], P('section', 'dp')
- grad_unite_weight: float32 [9, 336, 256], replicated
- grad_unite_gain: float32 [256], replicated
- grad_unite_bias: float32 [256], replicated
- grad_first_weight: float32 [4, 9, 256, 256], P('section')
- grad_second_weight: float32 [4, 9, 256, 256], P('section')
- grad_first_gain: float32 [4, 256], P('section')
- grad_first_bias: float32 [4, 256], P('section')
- grad_second_gain: float32 [4, 256], P('section')
- grad_second_bias: float32 [4, 256], P('section')
Inputs may be any that keep to these rules, and one draw needn't show every extreme that they name: `cell_index`: row-major index of a cell of the 16 x 16 grid.
All inputs are finite; a program needn't handle non-finite values.
Results may differ from a plain program's by a relative error of at most 0.03.
Values may be sent and summed in bfloat16 or wider, within the bound.
A program may use at most 192 MiB of HBM per device.

v0:
```python
import jax
import jax.numpy as jnp
from jax import lax
from jax.sharding import PartitionSpec as P

eps = 1e-05
pixel_block = 16


def shifted(value, axis, steps):
    count = lax.axis_size(axis)
    leading, last = (max(0, -steps), min(count, count - steps))
    return lax.ppermute(value, axis, [(source, source + steps) for source in range(leading, last)])


def from_root(block, axis, holder):
    block = jnp.where(lax.axis_index(axis) == holder, block, jnp.zeros_like(block))
    return lax.psum(block, axis)


def conv_apply(inputs, kernel):
    grid_size = inputs.shape[1]
    padded = jnp.pad(inputs, ((0, 0), (1, 1), (1, 1), (0, 0)))
    total = None
    for stencil in range(9):
        vertical, lateral = divmod(stencil, 3)
        window = padded[:, vertical : vertical + grid_size, lateral : lateral + grid_size]
        term = jnp.einsum(
            "nhwc,cd->nhwd", window, kernel[stencil], preferred_element_type=jnp.float32
        )
        total = term if total is None else total + term
    return total


def conv_back(grads, kernel):
    grid_size = grads.shape[1]
    padded = jnp.pad(grads, ((0, 0), (1, 1), (1, 1), (0, 0)))
    total = None
    for stencil in range(9):
        vertical, lateral = divmod(stencil, 3)
        window = padded[
            :, 2 - vertical : 2 - vertical + grid_size, 2 - lateral : 2 - lateral + grid_size
        ]
        term = jnp.einsum(
            "nhwd,cd->nhwc", window, kernel[stencil], preferred_element_type=jnp.float32
        )
        total = term if total is None else total + term
    return total


def conv_kernel_grad(inputs, grads):
    grid_size = inputs.shape[1]
    padded = jnp.pad(inputs, ((0, 0), (1, 1), (1, 1), (0, 0)))
    pieces = []
    for stencil in range(9):
        vertical, lateral = divmod(stencil, 3)
        window = padded[:, vertical : vertical + grid_size, lateral : lateral + grid_size]
        pieces.append(
            jnp.einsum("nhwc,nhwd->cd", window, grads, preferred_element_type=jnp.float32)
        )
    return jnp.stack(pieces)


def silu_slope(value):
    sigmoid_value = jax.nn.sigmoid(value)
    return sigmoid_value * (1.0 + value * (1.0 - sigmoid_value))


def expand(values):
    return values[:, None, None, None, :]


def bn_forward(activ, norm_count):
    center = lax.psum(jnp.sum(activ, axis=(1, 2, 3)), "dp") / norm_count
    offsets = activ - expand(center)
    spread = lax.psum(jnp.sum(offsets * offsets, axis=(1, 2, 3)), "dp") / norm_count
    return (center, lax.rsqrt(spread + eps))


def bn_backward(dnormed, normed, gain, scale, norm_count):
    first_sum, second_sum = lax.psum(
        (jnp.sum(dnormed, axis=(1, 2, 3)), jnp.sum(dnormed * normed, axis=(1, 2, 3))), "dp"
    )
    return (
        gain
        * expand(scale)
        * (dnormed - expand(first_sum / norm_count) - normed * expand(second_sum / norm_count))
    )


def store_slot(buffer, value, position, flag):
    previous = lax.dynamic_index_in_dim(buffer, position, 0, keepdims=False)
    return lax.dynamic_update_index_in_dim(buffer, jnp.where(flag, value, previous), position, 0)


def take_rows(table, where_rows):
    return jnp.take(table, where_rows, axis=0)


def lift_forward(context, logits, cells, cell_count):
    samples, pixels, bins = logits.shape
    probability = jax.nn.softmax(logits.astype(jnp.float32), axis=-1)
    points = (probability[..., None] * context.astype(jnp.float32)[:, :, None, :]).astype(
        jnp.bfloat16
    )
    block_pixels = min(pixels, pixel_block)
    blocks = pixels // block_pixels
    point_blocks = points.reshape(samples, blocks, block_pixels * bins, -1).transpose(1, 0, 2, 3)
    cell_blocks = cells.reshape(samples, blocks, block_pixels * bins).transpose(1, 0, 2)
    targets = lax.iota(jnp.int32, cell_count)

    def add_block(total, pieces):
        block_points, block_cells = pieces
        onehot = (block_cells[:, :, None] == targets[None, None, :]).astype(jnp.bfloat16)
        return (
            total
            + jnp.einsum("src,srk->sck", onehot, block_points, preferred_element_type=jnp.float32),
            None,
        )

    start = jnp.zeros((samples, cell_count, context.shape[-1]), jnp.float32)
    pooled, unused = lax.scan(add_block, start, (point_blocks, cell_blocks))
    return (probability, pooled)


def lift_backward(pooled_grad, probability, context, cells):
    samples, pixels, bins = probability.shape
    point_grad = jax.vmap(take_rows)(pooled_grad, cells.reshape(samples, pixels * bins)).reshape(
        samples, pixels, bins, -1
    )
    prob_grad = jnp.sum(point_grad * context.astype(jnp.float32)[:, :, None, :], axis=-1)
    context_grad = jnp.sum(point_grad * probability[..., None], axis=2)
    logit_grad = probability * (
        prob_grad - jnp.sum(prob_grad * probability, axis=-1, keepdims=True)
    )
    return (context_grad, logit_grad)


def uniting_forward(lidar, context, logits, cells, weight, gain, bias, norm_count):
    micro_count, samples, grid_size = (lidar.shape[0], lidar.shape[1], lidar.shape[2])
    flat = micro_count * samples
    probability, pooled = lift_forward(
        context.reshape(flat, context.shape[2], context.shape[3]),
        logits.reshape(flat, logits.shape[2], logits.shape[3]),
        cells.reshape(flat, cells.shape[2], cells.shape[3]),
        grid_size * grid_size,
    )
    joined = jnp.concatenate(
        [
            lidar.reshape(flat, grid_size, grid_size, lidar.shape[-1]),
            pooled.reshape(flat, grid_size, grid_size, -1).astype(jnp.bfloat16),
        ],
        axis=-1,
    )
    activ = conv_apply(joined, weight).reshape(micro_count, samples, grid_size, grid_size, -1)
    center, scale = bn_forward(activ, norm_count)
    normed = (activ - expand(center)) * expand(scale)
    preact = gain * normed + bias
    united = jax.nn.silu(preact).astype(jnp.bfloat16)
    return (united, (probability, joined, normed, preact, scale))


def uniting_backward(united_grad, saved, context, cells, weight, gain, norm_count, lidar_channels):
    probability, joined, normed, preact, scale = saved
    micro_count, samples, grid_size = (
        united_grad.shape[0],
        united_grad.shape[1],
        united_grad.shape[2],
    )
    flat = micro_count * samples
    dpreact = united_grad.astype(jnp.float32) * silu_slope(preact)
    gain_grad = jnp.sum(dpreact * normed, axis=(0, 1, 2, 3))
    bias_grad = jnp.sum(dpreact, axis=(0, 1, 2, 3))
    dactiv = (
        bn_backward(dpreact, normed, gain, scale, norm_count)
        .astype(jnp.bfloat16)
        .reshape(flat, grid_size, grid_size, -1)
    )
    weight_grad = conv_kernel_grad(joined, dactiv)
    joined_grad = conv_back(dactiv, weight)
    lidar_grad = joined_grad[..., :lidar_channels].reshape(
        micro_count, samples, grid_size, grid_size, lidar_channels
    )
    pooled_grad = joined_grad[..., lidar_channels:].reshape(flat, grid_size * grid_size, -1)
    context_grad, logit_grad = lift_backward(
        pooled_grad,
        probability,
        context.reshape(flat, context.shape[2], context.shape[3]),
        cells.reshape(flat, cells.shape[2], cells.shape[3]),
    )
    return (
        lidar_grad,
        context_grad.reshape(context.shape),
        logit_grad.reshape(cells.shape),
        weight_grad,
        gain_grad,
        bias_grad,
    )


def body(
    lidar,
    context,
    depth_logits,
    cell_index,
    unite_weight,
    unite_gain,
    unite_bias,
    first_weight,
    second_weight,
    first_gain,
    first_bias,
    second_gain,
    second_bias,
    cotangent,
):
    sections = lax.axis_size("section")
    section_index = lax.axis_index("section")
    micro_count = cotangent.shape[0]
    owned_count = lidar.shape[0]
    samples = lidar.shape[1]
    grid_size = lidar.shape[2]
    lidar_channels = lidar.shape[-1]
    channels = cotangent.shape[-1]
    norm_count = samples * grid_size * grid_size * lax.axis_size("dp")
    lidar_all, context_all, logits_all = (
        lax.all_gather(lidar, "section", axis=0, tiled=True),
        lax.all_gather(context, "section", axis=0, tiled=True),
        lax.all_gather(depth_logits, "section", axis=0, tiled=True),
    )
    cells_all = lax.all_gather(cell_index, "section", axis=0, tiled=True)
    united_all, saved = uniting_forward(
        lidar_all,
        context_all,
        logits_all,
        cells_all,
        unite_weight,
        unite_gain,
        unite_bias,
        norm_count,
    )
    kernel_one, kernel_two = (first_weight[0], second_weight[0])
    gain_one, bias_one = (first_gain[0], first_bias[0])
    gain_two, bias_two = (second_gain[0], second_bias[0])
    block_shape = (samples, grid_size, grid_size, channels)
    keep_input = jnp.zeros((micro_count,) + block_shape, jnp.bfloat16)
    keep_hidden = jnp.zeros((micro_count,) + block_shape, jnp.bfloat16)
    keep_first = jnp.zeros((micro_count,) + block_shape, jnp.float32)
    keep_second = jnp.zeros((micro_count,) + block_shape, jnp.float32)
    keep_stats = jnp.zeros((micro_count, 4, channels), jnp.float32)
    result_buffer = jnp.zeros((micro_count,) + block_shape, jnp.float32)
    received = jnp.zeros(block_shape, jnp.bfloat16)
    moments = micro_count + sections - 1
    for moment in range(moments):
        number = moment - section_index
        active = (number >= 0) & (number < micro_count)
        position = jnp.clip(number, 0, micro_count - 1)
        entering = lax.dynamic_index_in_dim(united_all, position, 0, keepdims=False)
        inputs = jnp.where(section_index == 0, entering, received)
        first_act = conv_apply(inputs, kernel_one)
        center_one, scale_one = bn_forward(first_act[None], norm_count)
        hidden = jax.nn.silu(
            gain_one * (first_act - center_one[0]) * scale_one[0] + bias_one
        ).astype(jnp.bfloat16)
        second_act = conv_apply(hidden, kernel_two)
        center_two, scale_two = bn_forward(second_act[None], norm_count)
        output = inputs.astype(jnp.float32) + jax.nn.silu(
            gain_two * (second_act - center_two[0]) * scale_two[0] + bias_two
        )
        keep_input = store_slot(keep_input, inputs, position, active)
        keep_hidden = store_slot(keep_hidden, hidden, position, active)
        keep_first = store_slot(keep_first, first_act, position, active)
        keep_second = store_slot(keep_second, second_act, position, active)
        keep_stats = store_slot(
            keep_stats,
            jnp.stack([center_one[0], scale_one[0], center_two[0], scale_two[0]]),
            position,
            active,
        )
        result_buffer = store_slot(
            result_buffer, output, position, active & (section_index == sections - 1)
        )
        if moment + 1 < moments:
            received = shifted(output.astype(jnp.bfloat16), "section", 1)
    grad_kernel_one = jnp.zeros(kernel_one.shape, jnp.float32)
    grad_kernel_two = jnp.zeros(kernel_two.shape, jnp.float32)
    grad_gain_one = jnp.zeros((channels,), jnp.float32)
    grad_bias_one = jnp.zeros((channels,), jnp.float32)
    grad_gain_two = jnp.zeros((channels,), jnp.float32)
    grad_bias_two = jnp.zeros((channels,), jnp.float32)
    united_grad_buffer = jnp.zeros((micro_count,) + block_shape, jnp.bfloat16)
    returned = jnp.zeros(block_shape, jnp.bfloat16)
    for moment in range(moments):
        number = moment - (sections - 1 - section_index)
        active = (number >= 0) & (number < micro_count)
        position = jnp.clip(number, 0, micro_count - 1)
        given = lax.dynamic_index_in_dim(cotangent, position, 0, keepdims=False).astype(jnp.float32)
        incoming = jnp.where(section_index == sections - 1, given, returned.astype(jnp.float32))
        incoming = jnp.where(active, incoming, 0.0)
        inputs = lax.dynamic_index_in_dim(keep_input, position, 0, keepdims=False)
        hidden = lax.dynamic_index_in_dim(keep_hidden, position, 0, keepdims=False)
        first_act = lax.dynamic_index_in_dim(keep_first, position, 0, keepdims=False)
        second_act = lax.dynamic_index_in_dim(keep_second, position, 0, keepdims=False)
        stats = lax.dynamic_index_in_dim(keep_stats, position, 0, keepdims=False)
        normed_two = (second_act - stats[2]) * stats[3]
        dpre_two = incoming * silu_slope(gain_two * normed_two + bias_two)
        grad_gain_two = grad_gain_two + jnp.sum(dpre_two * normed_two, axis=(0, 1, 2))
        grad_bias_two = grad_bias_two + jnp.sum(dpre_two, axis=(0, 1, 2))
        dsecond = bn_backward(
            dpre_two[None], normed_two[None], gain_two, stats[3][None], norm_count
        )[0].astype(jnp.bfloat16)
        grad_kernel_two = grad_kernel_two + conv_kernel_grad(hidden, dsecond)
        dhidden = conv_back(dsecond, kernel_two)
        normed_one = (first_act - stats[0]) * stats[1]
        dpre_one = dhidden * silu_slope(gain_one * normed_one + bias_one)
        grad_gain_one = grad_gain_one + jnp.sum(dpre_one * normed_one, axis=(0, 1, 2))
        grad_bias_one = grad_bias_one + jnp.sum(dpre_one, axis=(0, 1, 2))
        dfirst = bn_backward(
            dpre_one[None], normed_one[None], gain_one, stats[1][None], norm_count
        )[0].astype(jnp.bfloat16)
        grad_kernel_one = grad_kernel_one + conv_kernel_grad(inputs, dfirst)
        sending = (incoming + conv_back(dfirst, kernel_one)).astype(jnp.bfloat16)
        united_grad_buffer = store_slot(
            united_grad_buffer, sending, position, active & (section_index == 0)
        )
        if moment + 1 < moments:
            returned = shifted(sending, "section", -1)
    grad_kernel_one, grad_kernel_two, grad_gain_one, grad_bias_one, grad_gain_two, grad_bias_two = (
        lax.psum(
            (
                grad_kernel_one,
                grad_kernel_two,
                grad_gain_one,
                grad_bias_one,
                grad_gain_two,
                grad_bias_two,
            ),
            "dp",
        )
    )
    whole_result = from_root(result_buffer.astype(jnp.bfloat16), "section", sections - 1).astype(
        result_buffer.dtype
    )
    activations = lax.dynamic_slice_in_dim(
        whole_result, section_index * owned_count, owned_count, 0
    )
    united_grad_all = from_root(united_grad_buffer, "section", 0)
    lidar_whole, context_whole, logit_whole, unite_kernel_grad, unite_gain_grad, unite_bias_grad = (
        uniting_backward(
            united_grad_all,
            saved,
            context_all,
            cells_all,
            unite_weight,
            unite_gain,
            norm_count,
            lidar_channels,
        )
    )
    unite_kernel_grad, unite_gain_grad, unite_bias_grad = lax.psum(
        (unite_kernel_grad, unite_gain_grad, unite_bias_grad), "dp"
    )
    lidar_grad = lax.dynamic_slice_in_dim(lidar_whole, section_index * owned_count, owned_count, 0)
    context_grad = lax.dynamic_slice_in_dim(
        context_whole, section_index * owned_count, owned_count, 0
    )
    logit_grad = lax.dynamic_slice_in_dim(logit_whole, section_index * owned_count, owned_count, 0)
    return (
        activations,
        lidar_grad,
        context_grad,
        logit_grad,
        unite_kernel_grad,
        unite_gain_grad,
        unite_bias_grad,
        grad_kernel_one[None],
        grad_kernel_two[None],
        grad_gain_one[None],
        grad_bias_one[None],
        grad_gain_two[None],
        grad_bias_two[None],
    )


def solution(mesh):
    in_specs = (
        P("section", "dp", None, None, None),
        P("section", "dp", None, None),
        P("section", "dp", None, None),
        P("section", "dp", None, None),
        P(),
        P(),
        P(),
        P("section", None, None, None),
        P("section", None, None, None),
        P("section", None),
        P("section", None),
        P("section", None),
        P("section", None),
        P(None, "dp", None, None, None),
    )
    out_specs = (
        P("section", "dp", None, None, None),
        P("section", "dp", None, None, None),
        P("section", "dp", None, None),
        P("section", "dp", None, None),
        P(),
        P(),
        P(),
        P("section", None, None, None),
        P("section", None, None, None),
        P("section", None),
        P("section", None),
        P("section", None),
        P("section", None),
    )
    return jax.shard_map(body, mesh=mesh, in_specs=in_specs, out_specs=out_specs, check_vma=False)
```

profile of v0, /device:TPU:0, one launch (start us, length us, event | category | flops | bytes accessed | tf_op | source)
XLA Modules:
  0.0 2034.0 jit_solution(18354294024938461834)
XLA Ops:
  34.1 25.2 %reshape.4909 = f32[4,8,1888,80]{2,1,0,3:T(8,128)} reshape(f32[4,128,118,80]{2,1,0,3:T(8,128)} %mul.1880) | data formatting | bytes 38666240 | tf_op jit(solution)/shard_map/mul | solution.py:103
  89.5 28.8 %while.11 = (s32[]{:T(128)}, f32[4,256,80]{1,2,0:T(8,128)S(1)}, s32[8,4,1888]{2,0,1:T(8,128)S(1)}, bf16[8,4,1888,80]{2,3,1,0:T(8,128)(2,1)}, s32[]{:T(128)}, /*index=5*/s32[]{:T(128)}) while((s32[]{:T(128)}, f32[4,256,80]{1,2,0:T(8,128)S(1)}, s32[8,4,1888]{2,0,1:T(8,128)S(1)}, bf16[8,4,1888,80]{2,3,1,0:T(8,128)(2,1)}, s32[]{:T(128)}, ...), condition=%wide.region_3.4_spmd.clone, body=%wide.region_2.3_spmd.clone.sunk | while | flops 311427072 | bytes 2035295 | solution.py:122
  264.1 14.3 psum.503
  281.7 14.3 psum.504
  301.5 14.3 psum.505
  319.1 14.3 psum.506
  354.0 14.3 psum.507
  371.6 14.3 psum.508
  391.3 14.3 psum.509
  408.9 14.3 psum.510
  444.8 14.3 psum.511
  462.4 14.5 psum.512
  482.4 14.3 psum.513
  500.0 14.3 psum.514
  534.7 14.3 psum.515
  552.3 14.3 psum.516
  572.0 14.3 psum.517
  589.7 14.3 psum.518
  661.7 14.3 psum.521
  679.3 14.3 psum.522
  714.0 14.3 psum.523
  731.6 14.3 psum.524
  816.9 14.3 all-reduce.57
  971.5 14.3 all-reduce.51
  1024.8 14.3 all-reduce.49
  1077.3 14.3 all-reduce.47
  1176.1 41.1 %all-reduce.66.cloned.1.call-done = (bf16[4,1,16,16,256]{4,3,2,1,0:T(8,128)(2,1)}, bf16[4,1,16,16,256]{4,3,2,1,0:T(8,128)(2,1)}) async-done(((bf16[4,1,16,16,256]{4,3,2,1,0:T(8,128)(2,1)}, bf16[4,1,16,16,256]{4,3,2,1,0:T(8,128)(2,1)}), (bf16[4,1,16,16,256]{4,3,2,1,0:T(8,128)(2,1)}, bf16[4,1,16,16,256]{4,3,2,1,0:T(8,128)(2,1)})) %all-reduce.66.cloned.1.call-update) | async-done | bytes 1048592 | tf_op jit(solution)/shard_map/psum | solution.py:18
  1219.0 29.4 %all-reduce.44 = (f32[4,256]{1,0:T(4,128)S(1)}, f32[4,256]{1,0:T(4,128)S(1)}, f32[256]{0:T(256)}, f32[256]{0:T(256)}, f32[1,256]{1,0:T(1,128)}, /*index=5*/f32[1...) all-reduce(f32[4,256]{1,0:T(4,128)S(1)} %get-tuple-element.95, ...), channel_id=1, replica_groups=mesh['section'=4,'dp'=8] {'dp'}, use_global_device_ids=true, to_apply=%region_125.126 | all-reduce | flops 3584 | bytes 28672 | tf_op jit(solution)/shard_map/psum | solution.py:81
  1278.1 651.6 %gather_fusion = f32[60416,80]{1,0:T(8,128)} fusion(f32[4,256,80]{2,1,0:T(8,128)S(1)} %bitcast.3768, s32[60416]{0:T(1024)S(1)} %copy-done), kind=kCustom, calls=%fused_computation | custom fusion | bytes 39149568 | tf_op jit(solution)/shard_map/vmap(jit(_take))/gather | solution.py:97
  1929.8 25.9 %copy.98 = f32[60416,80]{0,1:T(8,128)} copy(f32[60416,80]{1,0:T(8,128)} %gather_fusion) | data formatting | bytes 38666240 | tf_op jit(solution)/shard_map/vmap(jit(_take))/gather | solution.py:97
  1955.7 44.6 %gather.7 = f32[4,128,118,80]{2,1,0,3:T(8,128)} reshape(f32[60416,80]{0,1:T(8,128)} %copy.98) | data formatting | bytes 38666240 | tf_op jit(solution)/shard_map/vmap(jit(_take))/gather | solution.py:97
  2000.3 14.6 multiply_reduce_fusion
  (1301 shorter events, 838.7 us)
Async XLA Ops:
  7.2 1210.1 %all-reduce.66.cloned.1.call-start = ((), (), s32[]{:S(2)}) async-start(), calls=%async_computation.1 | async-start | bytes 2097152 | tf_op jit(solution)/shard_map/psum | solution.py:18
  89.5 29.1 %copy-start.122 = (bf16[1,1,16,16,256]{4,3,2,1,0:T(8,128)(2,1)S(1)}, bf16[1,1,16,16,256]{4,3,2,1,0:T(8,128)(2,1)}, u32[]{:S(2)}) copy-start(bf16[1,1,16,16,256]{4,3,2,1,0:T(8,128)(2,1)} %param.16) | copy-start | bytes 393220
  132.1 29.6 %copy-start.243 = (f32[256]{0:T(256)S(1)}, f32[256]{0:T(256)}, u32[]{:S(2)}) copy-start(f32[256]{0:T(256)} %param.22) | copy-start | bytes 3076
  163.3 29.4 %copy-start.140 = (f32[1,256]{1,0:T(1,128)S(1)}, f32[1,256]{1,0:T(1,128)}, u32[]{:S(2)}) copy-start(f32[1,256]{1,0:T(1,128)} %param.25) | copy-start | bytes 3076
  163.4 29.4 %copy-start.143 = (f32[1,256]{1,0:T(1,128)S(1)}, f32[1,256]{1,0:T(1,128)}, u32[]{:S(2)}) copy-start(f32[1,256]{1,0:T(1,128)} %param.26) | copy-start | bytes 3076
  163.6 30.3 %copy-start.2 = (bf16[1,9,256,256]{3,2,1,0:T(8,128)(2,1)S(1)}, bf16[1,9,256,256]{3,2,1,0:T(8,128)(2,1)}, u32[]{:S(2)}) copy-start(bf16[1,9,256,256]{3,2,1,0:T(8,128)(2,1)} %param.24) | copy-start | bytes 3538948
  194.8 31.0 %copy-start.117 = (f32[1,256]{1,0:T(1,128)S(1)}, f32[1,256]{1,0:T(1,128)}, u32[]{:S(2)}) copy-start(f32[1,256]{1,0:T(1,128)} %param.27) | copy-start | bytes 3076
  194.8 30.9 %copy-start.118 = (f32[1,256]{1,0:T(1,128)S(1)}, f32[1,256]{1,0:T(1,128)}, u32[]{:S(2)}) copy-start(f32[1,256]{1,0:T(1,128)} %param.28) | copy-start | bytes 3076
  195.2 41.3 %copy-start.46 = (bf16[4,1,128,118]{3,2,0,1:T(8,128)(2,1)S(1)}, bf16[4,1,128,118]{3,2,0,1:T(8,128)(2,1)}, u32[]{:S(2)}) copy-start(bf16[4,1,128,118]{3,2,0,1:T(8,128)(2,1)} %copy-done.45) | copy-start | bytes 362500
  227.5 31.9 %collective-permute-start = (bf16[1,16,16,256]{3,2,1,0:T(8,128)(2,1)}, bf16[1,16,16,256]{3,2,1,0:T(8,128)(2,1)}, u32[]{:S(2)}, u32[]{:S(2)}) collective-permute-start(bf16[1,16,16,256]{3,2,1,0:T(8,128)(2,1)} %convert_bitcast_fusion), channel_id=1, source_target_pairs={{0,8},{8,16},{16,24},{1,9},{9,17},{17,25},{2,10},{10,18},{18,26},{... | collective-permute-start | bytes 393224 | tf_op jit(solution)/shard_map/ppermute | solution.py:13
  339.1 10.2 collective-permute-start.1
  428.9 11.2 collective-permute-start.2
  520.0 10.0 collective-permute-start.3
  609.6 10.0 collective-permute-start.4
  699.3 10.0 collective-permute-start.5
  837.4 9.6 collective-permute-start.6
  888.7 10.1 collective-permute-start.7
  939.8 10.2 collective-permute-start.8
  991.2 11.3 collective-permute-start.9
  1044.4 10.0 collective-permute-start.10
  1096.9 10.5 collective-permute-start.11
  1160.3 858.8 %all-reduce.64.cloned.1.call-start = ((), (), s32[]{:S(2)}) async-start(), calls=%async_computation | async-start | bytes 15630336 | tf_op jit(solution)/shard_map/psum | solution.py:360
  1171.7 45.6 %copy-start.4 = (f32[4,16,16,256]{3,2,1,0:T(8,128)S(1)}, f32[4,16,16,256]{3,2,1,0:T(8,128)}, u32[]{:S(2)}) copy-start(f32[4,16,16,256]{3,2,1,0:T(8,128)} %copy-done.3) | copy-start | bytes 3145732
  1171.7 45.6 %copy-start.139 = (f32[4,256]{1,0:T(4,128)S(1)}, f32[4,256]{1,0:T(4,128)}, u32[]{:S(2)}) copy-start(f32[4,256]{1,0:T(4,128)} %copy-done.138) | copy-start | bytes 12292
  1171.7 45.6 %copy-start.142 = (f32[4,256]{1,0:T(4,128)S(1)}, f32[4,256]{1,0:T(4,128)}, u32[]{:S(2)}) copy-start(f32[4,256]{1,0:T(4,128)} %copy-done.141) | copy-start | bytes 12292
  1171.7 45.6 %copy-start.202 = (f32[256]{0:T(256)S(1)}, f32[256]{0:T(256)}, u32[]{:S(2)}) copy-start(f32[256]{0:T(256)} %param.21) | copy-start | bytes 3076
  1171.7 45.6 %copy-start.244 = (f32[256]{0:T(256)S(1)}, f32[256]{0:T(256)}, u32[]{:S(2)}) copy-start(f32[256]{0:T(256)} %param.22) | copy-start | bytes 3076
  1176.1 72.3 %copy-start.200 = (f32[4,256]{1,0:T(4,128)S(1)}, f32[4,256]{1,0:T(4,128)}, u32[]{:S(2)}) copy-start(f32[4,256]{1,0:T(4,128)} %get-tuple-element.271) | copy-start | bytes 12292
  1955.7 44.6 %copy-start.81 = (f32[4,128,80]{1,0,2:T(4,128)S(1)}, f32[4,128,80]{1,0,2:T(4,128)}, u32[]{:S(2)}) copy-start(f32[4,128,80]{1,0,2:T(4,128)} %copy-done.80) | copy-start | bytes 491524
  1955.7 44.6 %copy-start.82 = (f32[4,128,118]{2,1,0:T(8,128)S(1)}, f32[4,128,118]{2,1,0:T(8,128)}, u32[]{:S(2)}) copy-start(f32[4,128,118]{2,1,0:T(8,128)} %fusion.273) | copy-start | bytes 724996
  1955.7 44.6 %copy-start.119 = (pred[4,128,118]{2,1,0:T(8,128)(4,1)S(1)}, pred[4,128,118]{2,1,0:T(8,128)(4,1)}, u32[]{:S(2)}) copy-start(pred[4,128,118]{2,1,0:T(8,128)(4,1)} %broadcast_in_dim.360) | copy-start | bytes 181252
  1955.7 44.6 %copy-start.120 = (pred[4,128,118]{2,1,0:T(8,128)(4,1)S(1)}, pred[4,128,118]{2,1,0:T(8,128)(4,1)}, u32[]{:S(2)}) copy-start(pred[4,128,118]{2,1,0:T(8,128)(4,1)} %copy.96) | copy-start | bytes 181252
  (259 other events, 1237.1 us)
Sparse Core Ops, SparseCore 0:
  1160.5 56.7 all-reduce.65
  1270.7 163.3 all-reduce.63
where the time goes:
time: 2050 us; the launch traced here: 2030 us
  local copies, waits for them, and re-layouts  867 us (42%)
  blocking collectives  686 us (33%)
  other arithmetic  204 us (10%)
  matrix products  193 us (9%)
  waiting for transfers between devices  41.5 us (2%)
  starting transfers between devices  23 us (1%)
    gather x4, local copies, waits for them, and re-layouts, take_rows(): return jnp.take(table, where_rows, axis=0)  724 us
    psum x15, blocking collectives, bn_backward(): lax.psum((jnp.sum(dnormed, axis=(1, 2, 3)), jnp.sum(dnormed * normed, axi...  224 us
    psum x15, blocking collectives, bn_forward(): lax.psum(jnp.sum(offsets * offsets, axis=(1, 2, 3)), 'dp') / norm_count  213 us
    psum x15, blocking collectives, bn_forward(): center = lax.psum(jnp.sum(activ, axis=(1, 2, 3)), 'dp') / norm_count  212 us
    dot_general x135, matrix products, conv_back(): jnp.einsum('nhwd,cd->nhwc', window, kernel[stencil], preferred_element_ty...  64.4 us
    dot_general x135, matrix products, conv_kernel_grad(): jnp.einsum('nhwc,nhwd->cd', window, grads, preferred_element_type=jnp.flo...  55.8 us
    dynamic_update_slice x36, other arithmetic, store_slot(): lax.dynamic_update_index_in_dim(buffer, jnp.where(flag, value, previous),...  47.9 us
    dynamic_slice x35, local copies, waits for them, and re-layouts, store_slot(): previous = lax.dynamic_index_in_dim(buffer, position, 0, keepdims=False)  47.9 us
  transfers between devices with their start and end apart: 14, of which 2 were waited for; matrix products, arithmetic and copies ran while one was open for 43% of the time, Pallas kernels for 0%

commit v1 on v0

v1 whole, which is shorter than its diff:
```python
import functools

import jax
import jax.numpy as jnp
from jax import lax
from jax.experimental import pallas as pl
from jax.experimental.pallas import tpu as pltpu
from jax.sharding import PartitionSpec as P

eps = 1e-05
f32, bf16 = jnp.float32, jnp.bfloat16
MESH = pl.DeviceIdType.MESH
side = 16
cells = side * side
transposed_rhs = (((1,), (1,)), ((), ()))
transposed_lhs = (((0,), (0,)), ((), ()))


def sigmoid(value):
    return 0.5 * jnp.tanh(0.5 * value) + 0.5


def slope(value):
    gate = sigmoid(value)
    return gate * (1.0 + value * (1.0 - gate))


def put_shifted(buffer, value, stride, offset=0):
    column = lax.broadcasted_iota(jnp.int32, (cells, 1), 0) % side
    width = value.shape[1]
    before = jnp.where(column == 0, 0.0, pltpu.roll(value, 1, 0))
    after = jnp.where(column == side - 1, 0.0, pltpu.roll(value, cells - 1, 0))
    for group, shifted in enumerate((before, value, after)):
        start = group * stride + offset
        buffer[side : side + cells, start : start + width] = shifted.astype(bf16)


def total_of(terms):
    total = None
    for term in terms:
        total = term if total is None else total + term
    return total


def conv(buffer, weight):
    return total_of(
        jnp.dot(buffer[side * i : side * i + cells, :], weight(i), preferred_element_type=f32) for i in range(3)
    )


def conv_transposed(buffer, weight, width):
    return total_of(
        lax.dot_general(
            buffer[side * (2 - i) : side * (2 - i) + cells, width * (2 - j) : width * (3 - j)],
            weight(3 * i + j),
            transposed_rhs,
            preferred_element_type=f32,
        )
        for i in range(3)
        for j in range(3)
    )


def kernel(
    peers,
    lidar_ref, context_ref, logit_ref, cell_ref, unite_ref, unite_gain, unite_bias, first_ref, second_ref,
    first_gain, first_bias, second_gain, second_bias, cotangent_ref,
    act_ref, lidar_grad, context_grad, logit_grad, unite_grad, first_grad, second_grad, sums_ref,
    joined, shifted, current, kept, normed, scales, held, mine, slots, probability, cell_wide, turned, histogram,
    send_sem, recv_sem,
):
    me = lax.axis_index("dp")
    blocks = first_ref.shape[0]
    channels = current.shape[1]
    bins = logit_ref.shape[1]
    cam = context_ref.shape[1]
    united_in = channels + cam
    count = float(peers * cells)

    barrier = pltpu.get_barrier_semaphore()
    for step in range(1, peers):
        pl.semaphore_signal(barrier, inc=1, device_id={"dp": lax.rem(me + step, peers)}, device_id_type=MESH)
    pl.semaphore_wait(barrier, peers - 1)

    def copy_stats(stage, step):
        return pltpu.make_async_remote_copy(
            src_ref=mine.at[stage], dst_ref=slots.at[stage, me], send_sem=send_sem.at[stage], recv_sem=recv_sem.at[stage],
            device_id={"dp": lax.rem(me + step, peers)}, device_id_type=MESH,
        )

    def send_stats(stage, first, second):
        mine[stage, 0:1] = first
        mine[stage, 1:2] = second
        slots[stage, me] = mine[stage]
        for step in range(1, peers):
            copy_stats(stage, step).start()

    def wait_peers(stage, semaphore):
        part = slots.at[stage, pl.ds(0, peers - 1)]
        pltpu.make_async_copy(part, part, semaphore.at[stage]).wait()

    def take_stats(stage):
        wait_peers(stage, recv_sem)
        return slots[stage, :, 0, :], slots[stage, :, 1, :]

    def local_moments(activ):
        center = jnp.sum(activ, axis=0, keepdims=True) * (1.0 / cells)
        offsets = activ - center
        return center, jnp.sum(offsets * offsets, axis=0, keepdims=True)

    def whole_moments(stage):
        centers, squares = take_stats(stage)
        center = jnp.sum(centers, axis=0, keepdims=True) * (1.0 / peers)
        apart = centers - center
        spread = jnp.sum(squares, axis=0, keepdims=True) + cells * jnp.sum(apart * apart, axis=0, keepdims=True)
        return center, lax.rsqrt(spread * (1.0 / count) + eps)

    def normalise(stage, activ, meanwhile):
        center, square = local_moments(activ)
        held[...] = activ
        send_stats(stage, center, square)
        meanwhile()
        center, scale = whole_moments(stage)
        value = (held[...] - center) * scale
        normed[stage] = value
        scales[stage] = scale
        return value

    def silu_of(value, gain, bias):
        pre = gain * value + bias
        return pre * sigmoid(pre)

    joined[...] = jnp.zeros_like(joined)
    shifted[...] = jnp.zeros_like(shifted)
    probability[...] = jnp.zeros_like(probability)
    cell_wide[...] = jnp.zeros_like(cell_wide)

    logits = logit_ref[...].astype(f32)
    raised = jnp.exp(logits - jnp.max(logits, axis=-1, keepdims=True))
    probability[:, 0:bins] = raised / jnp.sum(raised, axis=-1, keepdims=True)
    cell_wide[:, 0:bins] = cell_ref[...]
    turned[0] = probability[...].T
    turned[1] = cell_wide[...].astype(f32).T
    address = lax.broadcasted_iota(jnp.int32, (cells, 128), 0).astype(f32)

    def add_bin(number, total):
        return total + jnp.where(turned[1, pl.ds(number, 1)] == address, turned[0, pl.ds(number, 1)], 0.0)

    counted = lax.fori_loop(0, bins, add_bin, jnp.zeros((cells, 128), f32)).astype(bf16)
    histogram[...] = counted
    pooled = jnp.dot(counted, context_ref[...], preferred_element_type=f32)

    lidar = lidar_ref[...].astype(f32)
    put_shifted(joined, lidar, 384)
    put_shifted(joined, pooled, 384, channels)
    united = total_of(
        jnp.dot(
            joined[side * i : side * i + cells, 384 * j : 384 * j + united_in],
            unite_ref[united_in * (3 * i + j) : united_in * (3 * i + j + 1), :],
            preferred_element_type=f32,
        )
        for i in range(3)
        for j in range(3)
    )

    def keep_joined():
        kept[0, 0:channels] = lidar_ref[...].astype(f32).T.astype(bf16)
        wide = jnp.concatenate([pooled, jnp.zeros((cells, 128 - cam), f32)], axis=1)
        kept[0, channels : channels + 128] = wide.T.astype(bf16)

    value = normalise(0, united, keep_joined)
    entering = silu_of(value, unite_gain[...], unite_bias[...]).astype(bf16)
    current[...] = entering.astype(f32)

    def block(s, unused):
        stage = 2 * s + 1
        inputs = current[...]
        put_shifted(shifted, inputs, channels)
        activ = conv(shifted, lambda i: first_ref[s, 3 * channels * i : 3 * channels * (i + 1), :])

        def keep_inputs():
            kept[stage, 0:channels] = current[...].T.astype(bf16)

        value = normalise(stage, activ, keep_inputs)
        hidden = silu_of(value, first_gain[pl.ds(s, 1)], first_bias[pl.ds(s, 1)]).astype(bf16).astype(f32)
        put_shifted(shifted, hidden, channels)
        activ = conv(shifted, lambda i: second_ref[s, 3 * channels * i : 3 * channels * (i + 1), :])

        def keep_hidden():
            kept[stage + 1, 0:channels] = shifted[side : side + cells, channels : 2 * channels].astype(f32).T.astype(bf16)

        value = normalise(stage + 1, activ, keep_hidden)
        output = current[...] + silu_of(value, second_gain[pl.ds(s, 1)], second_bias[pl.ds(s, 1)])
        act_ref[...] = output
        current[...] = output.astype(bf16).astype(f32)
        return 0

    lax.fori_loop(0, blocks, block, 0)

    stages = 2 * blocks + 1

    def through_norm(stage, upstream, gain, bias, meanwhile):
        value = normed[stage]
        grads = upstream * slope(gain * value + bias)
        held[...] = grads
        send_stats(stages + stage, jnp.sum(grads, axis=0, keepdims=True), jnp.sum(grads * value, axis=0, keepdims=True))
        meanwhile()
        first, second = take_stats(stages + stage)
        first = jnp.sum(first, axis=0, keepdims=True)
        second = jnp.sum(second, axis=0, keepdims=True)
        sums_ref[stage, 0:1] = first
        sums_ref[stage, 1:2] = second
        result = (gain * scales[stage]) * (held[...] - first * (1.0 / count) - normed[stage] * (second * (1.0 / count)))
        put_shifted(shifted, result.astype(bf16).astype(f32), channels)

    def weight_grad(stage, store):
        for i in range(3):
            rows = shifted[side * (2 - i) : side * (2 - i) + cells, :]
            taps = jnp.dot(kept[stage, 0:channels], rows, preferred_element_type=f32).astype(bf16)
            for j in range(3):
                store(3 * i + j, taps[:, channels * (2 - j) : channels * (3 - j)])

    def store_first(s):
        def store(tap, value):
            first_grad[s, channels * tap : channels * (tap + 1), :] = value
        return store

    def store_second(s):
        def store(tap, value):
            second_grad[s, channels * tap : channels * (tap + 1), :] = value
        return store

    current[...] = cotangent_ref[...].astype(f32)

    def block_back(back, unused):
        s = blocks - 1 - back
        stage = 2 * s + 1

        def previous():
            @pl.when(back > 0)
            def _():
                weight_grad(stage + 2, store_first(s + 1))

        through_norm(stage + 1, current[...], second_gain[pl.ds(s, 1)], second_bias[pl.ds(s, 1)], previous)
        upstream = conv_transposed(
            shifted, lambda tap: second_ref[s, channels * tap : channels * (tap + 1), :], channels
        )
        through_norm(
            stage, upstream, first_gain[pl.ds(s, 1)], first_bias[pl.ds(s, 1)],
            lambda: weight_grad(stage + 1, store_second(s)),
        )
        passed = conv_transposed(
            shifted, lambda tap: first_ref[s, channels * tap : channels * (tap + 1), :], channels
        )
        current[...] = (current[...] + passed).astype(bf16).astype(f32)
        return 0

    lax.fori_loop(0, blocks, block_back, 0)

    through_norm(0, current[...], unite_gain[...], unite_bias[...], lambda: weight_grad(1, store_first(0)))
    lidar_grad[...] = conv_transposed(
        shifted, lambda tap: unite_ref[united_in * tap : united_in * tap + channels, :], channels
    )
    pooled_grad = conv_transposed(
        shifted, lambda tap: unite_ref[united_in * tap + channels : united_in * (tap + 1), :], channels
    ).astype(bf16)
    for i in range(3):
        rows = shifted[side * (2 - i) : side * (2 - i) + cells, :]
        taps = jnp.dot(kept[0, 0:united_in], rows, preferred_element_type=f32).astype(bf16)
        for j in range(3):
            tap = 3 * i + j
            unite_grad[united_in * tap : united_in * (tap + 1), :] = taps[:, channels * (2 - j) : channels * (3 - j)]

    context_grad[...] = lax.dot_general(histogram[...], pooled_grad, transposed_lhs, preferred_element_type=f32)
    table = lax.dot_general(context_ref[...], pooled_grad, transposed_rhs, preferred_element_type=f32)
    places = cell_wide[...]
    within = lax.rem(places, 128)
    low = jnp.take_along_axis(table[:, 0:128], within, axis=1)
    high = jnp.take_along_axis(table[:, 128:256], within, axis=1)
    chance = probability[...]
    chance_grad = jnp.where(places < 128, low, high)
    logits_grad = chance * (chance_grad - jnp.sum(chance_grad * chance, axis=-1, keepdims=True))
    logit_grad[...] = logits_grad[:, 0:bins]

    def drain(number, unused):
        wait_peers(number, send_sem)
        return 0

    lax.fori_loop(0, 2 * stages, drain, 0)


def body(
    lidar, context, depth_logits, cell_index, unite_weight, unite_gain, unite_bias, first_weight, second_weight,
    first_gain, first_bias, second_gain, second_bias, cotangent,
):
    peers = lax.axis_size("dp")
    section = lax.axis_index("section")
    channels = cotangent.shape[-1]
    pixels, bins = depth_logits.shape[2:]
    cam = context.shape[-1]
    united_in = unite_weight.shape[1]

    def gathered(array):
        return lax.all_gather(array, "section", axis=0, tiled=True)

    first_all = gathered(first_weight).reshape(-1, 9 * channels, channels)
    second_all = gathered(second_weight).reshape(-1, 9 * channels, channels)
    vectors = gathered(jnp.stack([first_gain, first_bias, second_gain, second_bias], axis=1))
    blocks = first_all.shape[0]
    stages = 2 * blocks + 1
    cot = lax.dynamic_index_in_dim(cotangent, section, 0, keepdims=False)

    vmem = pl.BlockSpec(memory_space=pltpu.VMEM)
    shape = jax.ShapeDtypeStruct
    act, lidar_grad, context_grad, logit_grad, unite_grad, first_grad, second_grad, sums = pl.pallas_call(
        functools.partial(kernel, peers),
        out_shape=(
            shape((cells, channels), f32),
            shape((cells, channels), f32),
            shape((pixels, cam), f32),
            shape((pixels, bins), f32),
            shape((9 * united_in, channels), bf16),
            shape((blocks, 9 * channels, channels), bf16),
            shape((blocks, 9 * channels, channels), bf16),
            shape((stages, 2, channels), f32),
        ),
        in_specs=[vmem] * 14,
        out_specs=[vmem] * 8,
        scratch_shapes=[
            pltpu.VMEM((cells + 2 * side, 3 * 384), bf16),
            pltpu.VMEM((cells + 2 * side, 3 * channels), bf16),
            pltpu.VMEM((cells, channels), f32),
            pltpu.VMEM((stages, 384, cells), bf16),
            pltpu.VMEM((stages, cells, channels), f32),
            pltpu.VMEM((stages, 1, channels), f32),
            pltpu.VMEM((cells, channels), f32),
            pltpu.VMEM((2 * stages, 2, channels), f32),
            pltpu.VMEM((2 * stages, peers, 2, channels), f32),
            pltpu.VMEM((128, 128), f32),
            pltpu.VMEM((128, 128), jnp.int32),
            pltpu.VMEM((2, 128, 128), f32),
            pltpu.VMEM((cells, 128), bf16),
            pltpu.SemaphoreType.DMA((2 * stages,)),
            pltpu.SemaphoreType.DMA((2 * stages,)),
        ],
        compiler_params=pltpu.CompilerParams(
            collective_id=0, has_side_effects=True, vmem_limit_bytes=60 << 20
        ),
    )(
        lidar.reshape(cells, channels), context.reshape(pixels, cam), depth_logits.reshape(pixels, bins),
        cell_index.reshape(pixels, bins), unite_weight.reshape(-1, channels),
        unite_gain[None], unite_bias[None], first_all, second_all,
        vectors[:, 0], vectors[:, 1], vectors[:, 2], vectors[:, 3], cot.reshape(cells, channels),
    )

    whole = lax.psum(unite_grad.astype(f32), ("section", "dp"))
    first_whole = lax.psum(lax.psum_scatter(first_grad.astype(f32), "section", scatter_dimension=0, tiled=True), "dp")
    second_whole = lax.psum(lax.psum_scatter(second_grad.astype(f32), "section", scatter_dimension=0, tiled=True), "dp")
    sums = lax.psum(sums, "section")
    own = lax.dynamic_slice_in_dim(sums[1:].reshape(blocks, 2, 2, channels), section, 1, 0)
    return (
        act.reshape(lidar.shape),
        lidar_grad.reshape(lidar.shape),
        context_grad.reshape(context.shape),
        logit_grad.reshape(depth_logits.shape),
        whole.reshape(unite_weight.shape),
        sums[0, 1],
        sums[0, 0],
        first_whole.reshape(first_weight.shape),
        second_whole.reshape(second_weight.shape),
        own[:, 0, 1],
        own[:, 0, 0],
        own[:, 1, 1],
        own[:, 1, 0],
    )


def solution(mesh):
    split, by_dp = P("section"), P("section", "dp")
    in_specs = (by_dp, by_dp, by_dp, by_dp, P(), P(), P(), split, split, split, split, split, split, P(None, "dp"))
    out_specs = (by_dp, by_dp, by_dp, by_dp, P(), P(), P(), split, split, split, split, split, split)
    return jax.shard_map(body, mesh=mesh, in_specs=in_specs, out_specs=out_specs, check_vma=False)
```

time: 2050 us -> 553 us (0.27)
  local copies, waits for them, and re-layouts: 867 us -> 13.6 us
  blocking collectives: 686 us -> 110 us
  waiting for transfers between devices: 41.5 us -> 305 us
  matrix products: 193 us -> 0 us
  other arithmetic: 204 us -> 13.9 us
  Pallas kernels: 0 us -> 96.9 us
  starting transfers between devices: 23 us -> 0.2 us
    gather x4 -> x0, local copies, waits for them, and re-layouts: 724 us -> none  [take_rows(): return jnp.take(table, where_rows, axis=0)]
    psum x45 -> x2, blocking collectives: 649 us -> 100 us  [the longest x1 84.7 us: body(): whole = lax.psum(unite_grad.astype(f32), ('section', 'dp'))]
    dot_general x413 -> x0, matrix products: 193 us -> none  [the longest x135 64.4 us: conv_back(): jnp.einsum('nhwd,cd->nhwc', window, kernel[stencil], preferred_element_ty...]
    unnamed x2 -> x7, waiting for transfers between devices: 0.03 us -> 185 us
    all_gather x0 -> x2, waiting for transfers between devices: none -> 106 us  [gathered(): return lax.all_gather(array, 'section', axis=0, tiled=True)]
    pallas_call x0 -> x1, Pallas kernels: none -> 96.9 us  [body(): pl.pallas_call(functools.partial(kernel, peers), out_shape=(shape((cells,...]
    reduce_sum x39 -> x0, other arithmetic: 54.8 us -> none  [the longest x15 20.5 us: bn_forward(): jnp.sum(offsets * offsets, axis=(1, 2, 3))]
    dynamic_slice x52 -> x1, local copies, waits for them, and re-layouts: 48.9 us -> 0.67 us  [body(): cot = lax.dynamic_index_in_dim(cotangent, section, 0, keepdims=False)]
  transfers between devices with their start and end apart: 14 -> 5, of which waited for: 2 -> 5; matrix products, arithmetic and copies ran while one was open for 43% -> 2% of each run, Pallas kernels for 0% -> 0%
where the time goes in v1:
time: 553 us
  waiting for transfers between devices  305 us (55%)
  blocking collectives  110 us (20%)
  Pallas kernels  96.9 us (18%)
  other arithmetic  13.9 us (3%)
  between operations  13.9 us (3%)
  local copies, waits for them, and re-layouts  13.6 us (2%)
    unnamed x7, waiting for transfers between devices  185 us
    all_gather x2, waiting for transfers between devices, gathered(): return lax.all_gather(array, 'section', axis=0, tiled=True)  106 us
    pallas_call x1, Pallas kernels, body(): pl.pallas_call(functools.partial(kernel, peers), out_shape=(shape((cells,...  96.9 us
    psum x1, blocking collectives, body(): whole = lax.psum(unite_grad.astype(f32), ('section', 'dp'))  84.7 us
    psum x1, blocking collectives, body(): sums = lax.psum(sums, 'section')  15.3 us
    psum x1, waiting for transfers between devices, body(): lax.psum(lax.psum_scatter(first_grad.astype(f32), 'section', scatter_dime...  13.8 us
  transfers between devices with their start and end apart: 5, of which 5 were waited for; matrix products, arithmetic and copies ran while one was open for 2% of the time, Pallas kernels for 0%

profile of v1, /device:TPU:0, one launch (start us, length us, event | category | flops | bytes accessed | tf_op | source)
XLA Modules:
  0.0 553.0 jit_solution(400276519828812703)
XLA Ops:
  7.3 0.7 all-gather.3.cloned.1.call-update
  8.0 0.0 all-gather.5.cloned.1.call-start
  8.0 0.7 all-gather.5.cloned.1.call-update
  8.8 0.0 reduce-scatter.7.cloned.1.call-start
  8.8 0.7 copy.34
  9.6 0.7 copy.32
  10.3 0.7 copy.33
  11.0 9.6 %all_gather.11 = f32[4,4,256]{2,1,0:T(4,128)S(1)} all-gather(f32[1,4,256]{2,1,0:T(4,128)S(1)} %pad_maximum_fusion), channel_id=1, replica_groups=mesh['section'=4,'dp'=8] {'section'}, dimensions={0}, use_global_device_ids=true | all-gather | bytes 20480 | tf_op jit(solution)/shard_map/all_gather | solution.py:304
  20.7 0.7 constant_dynamic-slice_fusion.4
  21.3 0.6 copy_bitcast_fusion
  21.9 0.6 copy_bitcast_fusion.2
  22.5 47.2 %all-gather.3.cloned.1.call-done = bf16[4,9,256,256]{3,2,1,0:T(8,128)(2,1)} async-done(((bf16[1,9,256,256]{3,2,1,0:T(8,128)(2,1)}), bf16[4,9,256,256]{3,2,1,0:T(8,128)(2,1)}) %all-gather.3.cloned.1.call-update) | async-done | bytes 4718608 | tf_op jit(solution)/shard_map/all_gather | solution.py:304
  69.7 58.9 %all-gather.5.cloned.1.call-done = bf16[4,9,256,256]{3,2,1,0:T(8,128)(2,1)} async-done(((bf16[1,9,256,256]{3,2,1,0:T(8,128)(2,1)}), bf16[4,9,256,256]{3,2,1,0:T(8,128)(2,1)}) %all-gather.5.cloned.1.call-update) | async-done | bytes 4718608 | tf_op jit(solution)/shard_map/all_gather | solution.py:304
  128.7 96.9 %shard_map.237 = (f32[256,256]{1,0:T(8,128)}, f32[256,256]{1,0:T(8,128)}, f32[128,80]{1,0:T(8,128)}, f32[128,118]{1,0:T(8,128)}, bf16[3024,256]{1,0:T(8,128)(2,1...) custom-call(bf16[256,256]{1,0:T(8,128)(2,1)} %bitcast.52, ...), custom_call_target="tpu_custom_call" | custom-call | tf_op jit(solution)/shard_map/pallas_call | solution.py:315
  225.6 6.8 %convert_element_type.10 = f32[4,2304,256]{2,1,0:T(8,128)} convert(bf16[4,2304,256]{2,1,0:T(8,128)(2,1)} %get-tuple-element.27) | non-fusion elementwise | flops 2359296 | bytes 14155776 | tf_op jit(solution)/shard_map/convert_element_type | solution.py:357
  232.5 0.0 reduce-scatter.9.cloned.1.call-start
  232.6 7.0 %convert_element_type.11 = f32[4,2304,256]{2,1,0:T(8,128)} convert(bf16[4,2304,256]{2,1,0:T(8,128)(2,1)} %get-tuple-element.28) | non-fusion elementwise | flops 2359296 | bytes 14155776 | tf_op jit(solution)/shard_map/convert_element_type | solution.py:358
  239.6 0.0 all-reduce.6.cloned.1.call-start
  239.6 85.5 %reduce-scatter.7.cloned.1.call-done = f32[1,2304,256]{2,1,0:T(8,128)} async-done(((f32[4,2304,256]{2,1,0:T(8,128)}), f32[1,2304,256]{2,1,0:T(8,128)}) %reduce-scatter.7.cloned.1.call-update) | async-done | bytes 2359312
  325.1 98.0 %reduce-scatter.9.cloned.1.call-done = f32[1,2304,256]{2,1,0:T(8,128)} async-done(((f32[4,2304,256]{2,1,0:T(8,128)}), f32[1,2304,256]{2,1,0:T(8,128)}) %reduce-scatter.9.cloned.1.call-update) | async-done | bytes 2359312
  423.2 0.7 copy-done.10
  423.9 15.3 %psum.29 = f32[9,2,256]{2,1,0:T(2,128)S(1)} all-reduce(f32[9,2,256]{2,1,0:T(2,128)S(1)} %copy-done.10), channel_id=1, replica_groups=mesh['section'=4,'dp'=8] {'section'}, use_global_device_ids=true, to_apply=%region_1.2 | all-reduce | flops 4608 | bytes 36864 | tf_op jit(solution)/shard_map/psum | solution.py:359
  439.1 0.7 copy.40
  439.9 0.7 copy.39
  440.6 0.6 fusion
  441.2 0.6 fusion.4
  441.7 84.7 %all-reduce.7 = f32[9,336,256]{2,1,0:T(8,128)} all-reduce(bf16[9,336,256]{2,1,0:T(8,128)(2,1)S(1)} %bitcast.47), channel_id=1, replica_groups=mesh['section'=4,'dp'=8] {'section','dp'}, use_global_device_ids=true, to_apply=%region_0.1 | all-reduce | flops 774144 | bytes 4644864 | tf_op jit(solution)/shard_map/psum | solution.py:356
  526.5 13.8 %all-reduce.6.cloned.1.call-done = (f32[1,9,256,256]{3,2,1,0:T(8,128)}, f32[1,9,256,256]{3,2,1,0:T(8,128)}) async-done(((f32[1,9,256,256]{3,2,1,0:T(8,128)}, f32[1,9,256,256]{3,2,1,0:T(8,128)}), (f32[1,9,256,256]{3,2,1,0:T(8,128)}, f32[1,9,256,256]{3,2,1,0:T(8,128)})) %all-reduce.6.cloned.1.call-update) | async-done | bytes 4718608 | tf_op jit(solution)/shard_map/psum | solution.py:357
  540.3 0.7 copy.55
  541.0 0.7 copy.56
  541.7 3.4 copy.57
  545.1 1.4 copy.58
  (36 shorter events, 0.2 us)
Async XLA Ops:
  7.2 13.5 %copy-start = (bf16[4,1,16,16,256]{4,3,2,1,0:T(8,128)(2,1)S(1)}, bf16[4,1,16,16,256]{4,3,2,1,0:T(8,128)(2,1)}, u32[]{:S(2)}) copy-start(bf16[4,1,16,16,256]{4,3,2,1,0:T(8,128)(2,1)} %param.27) | copy-start | bytes 1572868
  7.2 1.6 copy-start.7
  7.2 2.3 copy-start.9
  7.2 3.1 copy-start.8
  7.2 3.8 copy-start.13
  7.2 3.8 copy-start.12
  7.2 3.8 copy-start.11
  7.3 3.8 copy-start.14
  7.3 62.5 %all-gather.3.cloned.1.call-start = ((), (), s32[]{:S(2)}) async-start(), calls=%async_computation.2 | async-start | bytes 5898240 | tf_op jit(solution)/shard_map/all_gather | solution.py:304
  8.0 120.7 %all-gather.5.cloned.1.call-start = ((), (), s32[]{:S(2)}) async-start(), calls=%async_computation.3 | async-start | bytes 5898240 | tf_op jit(solution)/shard_map/all_gather | solution.py:304
  8.8 316.4 %reduce-scatter.7.cloned.1.call-start = ((), (), s32[]{:S(2)}) async-start(), calls=%async_computation.4 | async-start | bytes 11796480
  232.5 190.6 %reduce-scatter.9.cloned.1.call-start = ((), (), s32[]{:S(2)}) async-start(), calls=%async_computation.5 | async-start | bytes 11796480
  239.6 300.7 %all-reduce.6.cloned.1.call-start = ((), (), s32[]{:S(2)}) async-start(), calls=%async_computation.6 | async-start | bytes 9437184 | tf_op jit(solution)/shard_map/psum | solution.py:357
  423.2 0.7 copy-start.10
  423.2 16.0 %copy-start.5 = (f32[128,118]{1,0:T(8,128)S(1)}, f32[128,118]{1,0:T(8,128)}, u32[]{:S(2)}) copy-start(f32[128,118]{1,0:T(8,128)} %get-tuple-element.24) | copy-start | bytes 181252
  423.2 16.7 %copy-start.6 = (f32[128,80]{1,0:T(8,128)S(1)}, f32[128,80]{1,0:T(8,128)}, u32[]{:S(2)}) copy-start(f32[128,80]{1,0:T(8,128)} %get-tuple-element.23) | copy-start | bytes 122884
  423.2 18.6 %copy-start.2 = (bf16[3024,256]{1,0:T(8,128)(2,1)S(1)}, bf16[3024,256]{1,0:T(8,128)(2,1)}, u32[]{:S(2)}) copy-start(bf16[3024,256]{1,0:T(8,128)(2,1)} %get-tuple-element.25) | copy-start | bytes 4644868
  440.6 99.7 %copy-start.4 = (f32[256,256]{1,0:T(8,128)S(1)}, f32[256,256]{1,0:T(8,128)}, u32[]{:S(2)}) copy-start(f32[256,256]{1,0:T(8,128)} %get-tuple-element.21) | copy-start | bytes 786436
  441.7 99.3 %copy-start.3 = (f32[256,256]{1,0:T(8,128)S(1)}, f32[256,256]{1,0:T(8,128)}, u32[]{:S(2)}) copy-start(f32[256,256]{1,0:T(8,128)} %get-tuple-element.22) | copy-start | bytes 786436
  541.7 3.4 copy-start.1
Sparse Core Ops, SparseCore 0:
  9.9 59.7 all-gather.2
  71.6 57.0 all-gather.4
  232.6 92.4 reduce-scatter.6
  328.1 95.0 reduce-scatter.8
  425.4 114.8 all-reduce.5

commit v2 on v1

v2 whole, which is shorter than its diff:
```python
import functools

import jax
import jax.numpy as jnp
from jax import lax
from jax.experimental import pallas as pl
from jax.experimental.pallas import tpu as pltpu
from jax.sharding import PartitionSpec as P

eps = 1e-05
f32, bf16 = jnp.float32, jnp.bfloat16
MESH = pl.DeviceIdType.MESH
side = 16
cells = side * side
wide = 384
chips = 4
half = 128
flat_rows = 768
transposed_rhs = (((1,), (1,)), ((), ()))
transposed_lhs = (((0,), (0,)), ((), ()))


def sigmoid(value):
    return 0.5 * jnp.tanh(0.5 * value) + 0.5


def slope(value):
    gate = sigmoid(value)
    return gate * (1.0 + value * (1.0 - gate))


def silu(value):
    return value * sigmoid(value)


def put_shifted(buffer, value, stride, offset=0):
    column = lax.broadcasted_iota(jnp.int32, (cells, 1), 0) % side
    width = value.shape[1]
    before = jnp.where(column == 0, 0.0, pltpu.roll(value, 1, 0))
    after = jnp.where(column == side - 1, 0.0, pltpu.roll(value, cells - 1, 0))
    for group, shifted in enumerate((before, value, after)):
        start = group * stride + offset
        buffer[side : side + cells, start : start + width] = shifted.astype(bf16)


def total_of(terms):
    total = None
    for term in terms:
        total = term if total is None else total + term
    return total


def conv(buffer, weight):
    return total_of(
        jnp.dot(buffer[side * i : side * i + cells, :], weight(i), preferred_element_type=f32) for i in range(3)
    )


def conv_transposed(buffer, weight, width):
    return total_of(
        lax.dot_general(
            buffer[side * (2 - i) : side * (2 - i) + cells, width * (2 - j) : width * (3 - j)],
            weight(3 * i + j),
            transposed_rhs,
            preferred_element_type=f32,
        )
        for i in range(3)
        for j in range(3)
    )


def kernel(
    peers, sections,
    lidar_ref, context_ref, logit_ref, cell_ref, unite_ref, unite_gain, unite_bias, first_ref, second_ref,
    first_gain, first_bias, second_gain, second_bias, cotangent_ref,
    act_ref, lidar_grad, context_grad, logit_grad, unite_out, camera_out, first_out, second_out, sums_out,
    weights, unite_weight, vectors, joined, shifted, current, kept, normed, scales, held, gathered, upstream,
    lidars, cameras, mine, slots, unite_mine, unite_slots, probability, cell_wide, turned, histogram,
    partial, core_part, own_part, section_part, whole, flat, flat_core, flat_own, flat_section, flat_whole,
    totals, group_part, flat_group,
    local_sem, unite_send, unite_recv, stat_send, stat_recv, raw_send, raw_recv, cot_send, cot_recv,
    lidar_send, lidar_recv, camera_send, camera_recv, weight_send, weight_recv, relay_send, pass_send, pass_recv,
    vector_send, vector_recv, grad_send, grad_recv, total_send, total_recv, group_send, group_recv,
):
    me = lax.axis_index("dp")
    section = lax.axis_index("section")
    core = lax.rem(me, 2)
    chip = lax.rem(lax.div(me, 2), chips)
    group = lax.div(me, 2 * chips)
    groups = peers // (2 * chips)
    blocks = sections
    stages = 2 * blocks + 1
    channels = vectors.shape[-1]
    bins = logit_ref.shape[1]
    cam = context_ref.shape[1]
    united_in = channels + cam
    taken = 9 * channels
    row_half = lax.div(chip, 2)
    lane_half = lax.rem(chip, 2)
    count = float(peers * cells)

    def at(other_section=None, other=None):
        return (section if other_section is None else other_section, me if other is None else other)

    def chip_peer(step):
        return group * (2 * chips) + lax.rem(chip + step, chips) * 2 + core

    sibling = me + 1 - 2 * core

    def remote(source, target, send, recv, device):
        return pltpu.make_async_remote_copy(
            src_ref=source, dst_ref=target, send_sem=send, recv_sem=recv, device_id=device, device_id_type=MESH
        )

    def wait_for(part, semaphore):
        pltpu.make_async_copy(part, part, semaphore).wait()

    barrier = pltpu.get_barrier_semaphore()
    for step in range(1, sections):
        pl.semaphore_signal(
            barrier, inc=1, device_id=at(other_section=lax.rem(section + step, sections)), device_id_type=MESH
        )

    def greet(step, unused):
        pl.semaphore_signal(barrier, inc=1, device_id=at(other=lax.rem(me + step, peers)), device_id_type=MESH)
        return 0

    lax.fori_loop(1, peers, greet, 0)

    unite_copy = pltpu.make_async_copy(unite_ref, unite_weight, local_sem.at[0])
    own_first = pltpu.make_async_copy(first_ref, weights.at[2 * section], local_sem.at[1])
    own_second = pltpu.make_async_copy(second_ref, weights.at[2 * section + 1], local_sem.at[2])
    own_cot = pltpu.make_async_copy(cotangent_ref.at[section], upstream.at[chip], local_sem.at[3])
    own_lidar = pltpu.make_async_copy(lidar_ref, lidars.at[chip], local_sem.at[4])
    own_lidar.start()
    unite_copy.start()
    own_first.start()
    own_second.start()
    own_cot.start()
    for number, part in enumerate((first_gain, first_bias, second_gain, second_bias)):
        vectors[section, number : number + 1] = part[...]
    joined[...] = jnp.zeros_like(joined)
    probability[...] = jnp.zeros_like(probability)
    cell_wide[...] = jnp.zeros_like(cell_wide)
    cameras[chip] = jnp.zeros((cells, half), bf16)
    pl.semaphore_wait(barrier, peers - 1 + sections - 1)

    beside = section + 1 - 2 * lax.rem(section, 2)
    across = lax.rem(section + 2, sections)
    near = beside + core * (across - beside)
    far = across + core * (beside - across)
    part_rows = taken // 2
    part = pl.ds(pl.multiple_of(core * part_rows, part_rows), part_rows)
    sources = (first_ref, second_ref)

    def offer(which, target, number):
        index = 2 * section + which
        remote(
            sources[which].at[part], weights.at[index, part], weight_send.at[number], weight_recv.at[index],
            at(other_section=target),
        ).start()

    def arrived(index):
        wait_for(weights.at[index, part], weight_recv.at[index])

    def pass_on(index):
        remote(
            weights.at[index, part], weights.at[index, part], pass_send.at[index], pass_recv.at[index],
            at(other=sibling),
        ).start()

    def relay(block, which):
        index = 2 * block + which

        @pl.when(near == block)
        def _():
            arrived(index)
            remote(
                weights.at[index, part], weights.at[index, part], relay_send.at[which], weight_recv.at[index],
                at(other_section=far),
            ).start()
            pass_on(index)

    def arrive(block, which):
        index = 2 * block + which

        @pl.when((section != block) & (near != block))
        def _():
            arrived(index)
            pass_on(index)

    def ready(block, which):
        index = 2 * block + which
        rest = pl.ds(pl.multiple_of((1 - core) * part_rows, part_rows), part_rows)

        @pl.when(section != block)
        def _():
            wait_for(weights.at[index, rest], pass_recv.at[index])

        @pl.when(section == block)
        def _():
            (own_second if which else own_first).wait()

    offer(0, near, 0)
    for step in range(1, sections):
        remote(
            vectors.at[section], vectors.at[section], vector_send, vector_recv,
            at(other_section=lax.rem(section + step, sections)),
        ).start()

    logits = logit_ref[...].astype(f32)
    raised = jnp.exp(logits - jnp.max(logits, axis=-1, keepdims=True))
    probability[:, 0:bins] = raised / jnp.sum(raised, axis=-1, keepdims=True)
    cell_wide[:, 0:bins] = cell_ref[...]
    turned[0] = probability[...].T
    turned[1] = cell_wide[...].astype(f32).T
    address = lax.broadcasted_iota(jnp.int32, (cells, half), 0).astype(f32)

    def add_bin(number, total):
        return total + jnp.where(turned[1, pl.ds(number, 1)] == address, turned[0, pl.ds(number, 1)], 0.0)

    counted = lax.fori_loop(0, bins, add_bin, jnp.zeros((cells, half), f32)).astype(bf16)
    histogram[...] = counted
    pooled = jnp.dot(counted, context_ref[...], preferred_element_type=f32)
    cameras[chip, :, 0:cam] = pooled.astype(bf16)

    own_lidar.wait()
    put_shifted(joined, lidars[chip].astype(f32), wide)
    put_shifted(joined, pooled, wide, channels)
    unite_copy.wait()
    united = total_of(
        jnp.dot(
            joined[side * i : side * i + cells, wide * j : wide * j + united_in],
            unite_weight[united_in * (3 * i + j) : united_in * (3 * i + j + 1), :],
            preferred_element_type=f32,
        )
        for i in range(3)
        for j in range(3)
    )
    gathered[chip] = united.astype(bf16)
    for step in range(1, chips):
        remote(
            gathered.at[chip], gathered.at[chip], raw_send.at[step], raw_recv.at[step], at(other=chip_peer(step))
        ).start()
    center = jnp.sum(united, axis=0, keepdims=True) * (1.0 / cells)
    offsets = united - center
    unite_mine[0:1] = center
    unite_mine[1:2] = jnp.sum(offsets * offsets, axis=0, keepdims=True)
    unite_slots[me] = unite_mine[...]

    def send_unite(step, unused):
        remote(
            unite_mine, unite_slots.at[me], unite_send, unite_recv, at(other=lax.rem(me + step, peers))
        ).start()
        return 0

    lax.fori_loop(1, peers, send_unite, 0)

    @pl.when(section == 0)
    def _():
        offer(0, far, 1)
        offer(1, near, 2)

    shifted[...] = jnp.zeros_like(shifted)
    flat[9 * cam :, :] = jnp.zeros((flat_rows - 9 * cam, half), bf16)

    def merged(centers, squares, each):
        parts = centers.shape[0]
        center = jnp.sum(centers, axis=0, keepdims=True) * (1.0 / parts)
        apart = centers - center
        square = jnp.sum(squares, axis=0, keepdims=True) + each * jnp.sum(apart * apart, axis=0, keepdims=True)
        return center, square

    wait_for(unite_slots.at[pl.ds(0, peers - 1)], unite_recv)
    center, square = merged(unite_slots[:, 0, :], unite_slots[:, 1, :], cells)
    scales[0] = lax.rsqrt(square * (1.0 / count) + eps)
    scales[stages] = center
    relay(0, 0)

    @pl.when(section != 0)
    def _():
        offer(0, far, 1)

    def enter(number):
        value = (gathered[number].astype(f32) - scales[stages]) * scales[0]
        normed[0, number] = value
        entering = silu(unite_gain[...] * value + unite_bias[...])
        current[number] = entering.astype(bf16)
        kept[0, number] = entering.astype(bf16)
        put_shifted(shifted.at[number], entering, channels)

    enter(chip)
    for step in (1, 3, 2):
        wait_for(gathered.at[0], raw_recv.at[step])
        enter(lax.rem(chip - step + chips, chips))
        if step == 1:
            relay(1, 0)

            @pl.when(section == 0)
            def _():
                offer(1, far, 3)

    own_cot.wait()
    for step in range(1, chips):
        peer = at(other=chip_peer(step))
        remote(upstream.at[chip], upstream.at[chip], cot_send.at[step], cot_recv.at[step], peer).start()
    for step in range(1, chips):
        peer = at(other=chip_peer(step))
        remote(lidars.at[chip], lidars.at[chip], lidar_send.at[step], lidar_recv.at[step], peer).start()
        remote(cameras.at[chip], cameras.at[chip], camera_send.at[step], camera_recv.at[step], peer).start()

    arrive(0, 0)
    relay(0, 1)

    @pl.when(section != 0)
    def _():
        offer(1, near, 2)

    wait_for(vectors.at[pl.ds(0, sections - 1)], vector_recv)

    members = 2 * groups
    place = group * 2 + core

    def copy_stats(event, step):
        to = lax.rem(place + step, members)
        return remote(
            mine.at[event], slots.at[event, place], stat_send.at[event], stat_recv.at[event],
            at(other=lax.div(to, 2) * (2 * chips) + chip * 2 + lax.rem(to, 2)),
        )

    def send_stats(event, first, second):
        mine[event, 0:1] = first
        mine[event, 1:2] = second
        slots[event, place] = mine[event]
        for step in range(1, members):
            copy_stats(event, step).start()

    def take_stats(event):
        wait_for(slots.at[event, pl.ds(0, members - 1)], stat_recv.at[event])
        return slots[event, :, 0, :], slots[event, :, 1, :]

    def forward_stage(stage, weight, meanwhile, use):
        centers, squares = [], []
        for number in range(chips):
            activ = conv(shifted.at[number], weight)
            held[number] = activ
            center = jnp.sum(activ, axis=0, keepdims=True) * (1.0 / cells)
            offsets = activ - center
            centers.append(center)
            squares.append(jnp.sum(offsets * offsets, axis=0, keepdims=True))
        center, square = merged(jnp.concatenate(centers, axis=0), jnp.concatenate(squares, axis=0), cells)
        send_stats(stage - 1, center, square)
        meanwhile()
        centers, squares = take_stats(stage - 1)
        center, square = merged(centers, squares, chips * cells)
        scale = lax.rsqrt(square * (1.0 / count) + eps)
        scales[stage] = scale
        for number in range(chips):
            value = (held[number] - center) * scale
            normed[stage, number] = value
            use(number, value)

    def block(s, unused):
        stage = 2 * s + 1

        def vector(number):
            return vectors[s, number : number + 1]

        def during_first():
            @pl.when(s == 0)
            def _():
                relay(2, 0)

                @pl.when(section != 0)
                def _():
                    offer(1, far, 3)

            @pl.when(s == 1)
            def _():
                relay(2, 1)

            arrive(s, 1)

        def during_second():
            @pl.when(s == 0)
            def _():
                relay(3, 0)
                relay(1, 1)

            @pl.when(s == 1)
            def _():
                relay(3, 1)

            @pl.when(s < blocks - 1)
            def _():
                arrive(s + 1, 0)

        def use_first(number, value):
            hidden = silu(vector(0) * value + vector(1))
            kept[stage, number] = hidden.astype(bf16)
            put_shifted(shifted.at[number], hidden, channels)

        def use_second(number, value):
            output = current[number].astype(f32) + silu(vector(2) * value + vector(3))
            held[number] = output
            current[number] = output.astype(bf16)

            @pl.when(s < blocks - 1)
            def _():
                kept[stage + 1, number] = output.astype(bf16)
                put_shifted(shifted.at[number], output, channels)

        ready(s, 0)
        forward_stage(
            stage, lambda i: weights[2 * s, 3 * channels * i : 3 * channels * (i + 1), :], during_first, use_first
        )
        ready(s, 1)
        forward_stage(
            stage + 1, lambda i: weights[2 * s + 1, 3 * channels * i : 3 * channels * (i + 1), :],
            during_second, use_second,
        )
        return 0

    lax.fori_loop(0, blocks, block, 0)
    act_ref[...] = held[chip]

    rows16 = pl.ds(pl.multiple_of(section * 16, 16), 16)
    lanes = pl.ds(pl.multiple_of(lane_half * half, half), half)
    flat48 = pl.ds(pl.multiple_of(section * 48, 16), 48)

    def lateral(j):
        return pl.ds(pl.multiple_of(channels * (2 - j) + lane_half * half, half), half)

    def weight_grad(stage, inputs):
        columns = pl.ds(pl.multiple_of(row_half * half, half), half)
        values = [inputs[number, :, columns] for number in range(chips)]
        for i in range(3):
            for j in range(3):
                taps = total_of(
                    lax.dot_general(
                        values[number],
                        shifted[number, side * (2 - i) : side * (2 - i) + cells, lateral(j)],
                        transposed_lhs,
                        preferred_element_type=f32,
                    )
                    for number in range(chips)
                ).astype(bf16)
                partial[stage, 3 * i + j, 0] = taps[0:64]
                partial[stage, 3 * i + j, 1] = taps[64:128]
        to_sibling(stage)

    def to_sibling(k):
        remote(
            partial.at[k, :, 1 - core], core_part.at[k], grad_send.at[0, k], grad_recv.at[0, k], at(other=sibling)
        ).start()

    def to_sections(k):
        wait_for(core_part.at[k], grad_recv.at[0, k])
        for tap in range(9):
            own_part[k, tap] = (partial[k, tap, core].astype(f32) + core_part[k, tap].astype(f32)).astype(bf16)
        section_part[k, section] = own_part[k, :, rows16]
        for step in range(1, sections):
            other = lax.rem(section + step, sections)
            remote(
                own_part.at[k, :, pl.ds(pl.multiple_of(other * 16, 16), 16)], section_part.at[k, section],
                grad_send.at[1, k], grad_recv.at[1, k], at(other_section=other),
            ).start()

    def over_groups(k, value, buffer, number):
        if groups == 1:
            return value
        buffer[k, group] = value
        for step in range(1, groups):
            to = lax.rem(group + step, groups) * (2 * chips) + chip * 2 + core
            remote(
                buffer.at[k, group], buffer.at[k, group], group_send.at[number], group_recv.at[number], at(other=to)
            ).start()
        wait_for(buffer.at[k, pl.ds(0, groups - 1)], group_recv.at[number])
        return jnp.sum(buffer[k].astype(f32), axis=0).astype(bf16)

    def to_column(k):
        wait_for(section_part.at[k, pl.ds(0, sections - 1)], grad_recv.at[1, k])
        piece = total_of(section_part[k, number].astype(f32) for number in range(sections)).astype(bf16)
        place = whole.at[k, :, row_half, core, rows16, lanes]
        place[...] = over_groups(k, piece, group_part, k)
        for step in range(1, chips):
            remote(place, place, grad_send.at[2, k], grad_recv.at[2, k], at(other=chip_peer(step))).start()

    def column_arrived(k):
        wait_for(whole.at[k, :, 0, 0, pl.ds(0, 16 * (chips - 1)), pl.ds(0, half)], grad_recv.at[2, k])

    def to_owner(k, block):
        column_arrived(k)
        place = whole.at[k, :, :, core, rows16]

        @pl.when(section != block)
        def _():
            remote(place, place, grad_send.at[3, k], grad_recv.at[3, k], at(other_section=block)).start()

    def to_all(k):
        column_arrived(k)
        place = whole.at[k, :, :, core, rows16]
        for step in range(1, sections):
            other = lax.rem(section + step, sections)
            remote(place, place, grad_send.at[3, k], grad_recv.at[3, k], at(other_section=other)).start()

    def share(k):
        wait_for(whole.at[k, :, :, 0, pl.ds(0, 16 * (sections - 1))], grad_recv.at[3, k])
        place = whole.at[k, :, :, core]
        remote(place, place, grad_send.at[4, k], grad_recv.at[4, k], at(other=sibling)).start()

    def owner_share(k, block):
        @pl.when(section == block)
        def _():
            share(k)

    def shared(k):
        wait_for(whole.at[k, :, :, 0], grad_recv.at[4, k])

    def block_of(k):
        return lax.div(k - 1, 2)

    def advance(slot):
        due = ((2, to_sections), (4, to_column), (6, lambda k: to_owner(k, block_of(k))),
               (8, lambda k: owner_share(k, block_of(k))))
        for ahead, act in due:
            @pl.when(slot + ahead <= stages - 1)
            def _():
                act(slot + ahead)

    def backward_stage(stage, gain, bias, gradient, meanwhile):
        event = stages - 1 + stage
        firsts, seconds = None, None
        for number in range(chips):
            value = normed[stage, number]
            grads = gradient(number) * slope(gain * value + bias)
            held[number] = grads
            first = jnp.sum(grads, axis=0, keepdims=True)
            second = jnp.sum(grads * value, axis=0, keepdims=True)
            firsts = first if firsts is None else firsts + first
            seconds = second if seconds is None else seconds + second
        send_stats(event, firsts, seconds)
        meanwhile()
        first, second = take_stats(event)
        first = jnp.sum(first, axis=0, keepdims=True)
        second = jnp.sum(second, axis=0, keepdims=True)
        totals[section, stage, 0:1] = first
        totals[section, stage, 1:2] = second
        first = first * (1.0 / count)
        second = second * (1.0 / count)
        factor = gain * scales[stage]
        for number in range(chips):
            put_shifted(
                shifted.at[number], factor * (held[number] - first - normed[stage, number] * second), channels
            )

    for step in range(1, chips):
        wait_for(upstream.at[0], cot_recv.at[step])
        wait_for(upstream.at[0], cot_send.at[step])

    def block_back(back, unused):
        s = blocks - 1 - back
        stage = 2 * s + 1

        def vector(number):
            return vectors[s, number : number + 1]

        def during_second():
            @pl.when(back > 0)
            def _():
                weight_grad(stage + 2, kept.at[stage + 1])
            advance(stage + 1)

        def during_first():
            weight_grad(stage + 1, kept.at[stage])
            advance(stage)

        backward_stage(stage + 1, vector(2), vector(3), lambda number: upstream[number].astype(f32), during_second)
        for number in range(chips):
            held[number] = conv_transposed(
                shifted.at[number], lambda tap: weights[2 * s + 1, channels * tap : channels * (tap + 1), :], channels
            )
        backward_stage(stage, vector(0), vector(1), lambda number: held[number], during_first)
        for number in range(chips):
            passed = conv_transposed(
                shifted.at[number], lambda tap: weights[2 * s, channels * tap : channels * (tap + 1), :], channels
            )
            upstream[number] = (upstream[number].astype(f32) + passed).astype(bf16)
        return 0

    lax.fori_loop(0, blocks, block_back, 0)

    def during_unite():
        weight_grad(1, kept.at[0])
        advance(0)

    backward_stage(
        0, unite_gain[...], unite_bias[...], lambda number: upstream[number].astype(f32), during_unite
    )
    for step in range(1, sections):
        remote(
            totals.at[section], totals.at[section], total_send, total_recv,
            at(other_section=lax.rem(section + step, sections)),
        ).start()
    for step in range(1, chips):
        wait_for(lidars.at[0], lidar_recv.at[step])
        wait_for(cameras.at[0], camera_recv.at[step])
    weight_grad(0, lidars)
    held_cameras = [cameras[number] for number in range(chips)]
    for i in range(3):
        for j in range(3):
            taps = total_of(
                lax.dot_general(
                    held_cameras[number],
                    shifted[number, side * (2 - i) : side * (2 - i) + cells, lateral(j)],
                    transposed_lhs,
                    preferred_element_type=f32,
                )
                for number in range(chips)
            ).astype(bf16)
            flat[cam * (3 * i + j) : cam * (3 * i + j + 1)] = taps[0:cam]
    quarter = flat_rows // 4
    kept_rows = pl.ds(pl.multiple_of(row_half * (2 * quarter) + core * quarter, 16), quarter)
    sent_rows = pl.ds(pl.multiple_of(row_half * (2 * quarter) + (1 - core) * quarter, 16), quarter)
    extra = stages
    remote(
        flat.at[sent_rows], flat_core, grad_send.at[0, extra], grad_recv.at[0, extra], at(other=sibling)
    ).start()
    advance(-1)
    own = shifted.at[chip]
    lidar_grad[...] = conv_transposed(
        own, lambda tap: unite_weight[united_in * tap : united_in * tap + channels, :], channels
    )
    pooled_grad = conv_transposed(
        own, lambda tap: unite_weight[united_in * tap + channels : united_in * (tap + 1), :], channels
    ).astype(bf16)

    wait_for(flat_core, grad_recv.at[0, extra])
    flat_own[...] = (flat[kept_rows].astype(f32) + flat_core[...].astype(f32)).astype(bf16)
    flat_section[section] = flat_own[flat48]
    for step in range(1, sections):
        other = lax.rem(section + step, sections)
        remote(
            flat_own.at[pl.ds(pl.multiple_of(other * 48, 16), 48)], flat_section.at[section],
            grad_send.at[1, extra], grad_recv.at[1, extra], at(other_section=other),
        ).start()
    advance(-2)

    context_grad[...] = lax.dot_general(histogram[...], pooled_grad, transposed_lhs, preferred_element_type=f32)
    table = lax.dot_general(context_ref[...], pooled_grad, transposed_rhs, preferred_element_type=f32)
    places = cell_wide[...]
    within = lax.rem(places, half)
    low = jnp.take_along_axis(table[:, 0:half], within, axis=1)
    high = jnp.take_along_axis(table[:, half : 2 * half], within, axis=1)
    chance = probability[...]
    chance_grad = jnp.where(places < half, low, high)
    logits_grad = chance * (chance_grad - jnp.sum(chance_grad * chance, axis=-1, keepdims=True))
    logit_grad[...] = logits_grad[:, 0:bins]

    to_column(1)
    to_owner(3, 1)
    owner_share(5, 2)
    to_column(0)
    wait_for(flat_section.at[pl.ds(0, sections - 1)], grad_recv.at[1, extra])
    piece = total_of(flat_section[number].astype(f32) for number in range(sections)).astype(bf16)
    flat_place = flat_whole.at[row_half, core, flat48, lanes]
    flat_place[...] = over_groups(0, piece, flat_group, extra)
    for step in range(1, chips):
        remote(
            flat_place, flat_place, grad_send.at[2, extra], grad_recv.at[2, extra], at(other=chip_peer(step))
        ).start()
    to_owner(2, 0)
    owner_share(4, 1)
    to_owner(1, 0)
    owner_share(3, 1)
    to_all(0)
    wait_for(flat_whole.at[0, 0, pl.ds(0, 48 * (chips - 1)), pl.ds(0, half)], grad_recv.at[2, extra])
    flat_rows_place = flat_whole.at[:, core, flat48]
    for step in range(1, sections):
        other = lax.rem(section + step, sections)
        remote(
            flat_rows_place, flat_rows_place, grad_send.at[3, extra], grad_recv.at[3, extra],
            at(other_section=other),
        ).start()
    owner_share(2, 0)
    owner_share(1, 0)
    share(0)
    wait_for(flat_whole.at[:, 0, pl.ds(0, 48 * (sections - 1))], grad_recv.at[3, extra])
    flat_half = flat_whole.at[:, core]
    remote(flat_half, flat_half, grad_send.at[4, extra], grad_recv.at[4, extra], at(other=sibling)).start()

    wait_for(totals.at[pl.ds(0, sections - 1)], total_recv)
    sums_out[...] = total_of(totals[number] for number in range(sections))
    shared(2 * section + 1)
    shared(2 * section + 2)
    first_copy = pltpu.make_async_copy(whole.at[2 * section + 1], first_out, local_sem.at[5])
    second_copy = pltpu.make_async_copy(whole.at[2 * section + 2], second_out, local_sem.at[6])
    first_copy.start()
    second_copy.start()
    shared(0)
    unite_done = pltpu.make_async_copy(whole.at[0], unite_out, local_sem.at[7])
    unite_done.start()
    wait_for(flat_whole.at[:, 0], grad_recv.at[4, extra])
    camera_done = pltpu.make_async_copy(flat_whole, camera_out, local_sem.at[8])
    camera_done.start()

    wait_for(unite_slots.at[pl.ds(0, peers - 1)], unite_send)
    for step in range(1, chips):
        wait_for(gathered.at[0], raw_send.at[step])
        wait_for(lidars.at[0], lidar_send.at[step])
        wait_for(cameras.at[0], camera_send.at[step])
    for number in range(4):
        wait_for(weights.at[0, part], weight_send.at[number])
    for number in range(2):
        wait_for(weights.at[0, part], relay_send.at[number])
    wait_for(vectors.at[pl.ds(0, sections - 1)], vector_send)
    wait_for(totals.at[pl.ds(0, sections - 1)], total_send)

    def drain_stats(event, unused):
        wait_for(slots.at[event, pl.ds(0, members - 1)], stat_send.at[event])
        return 0

    lax.fori_loop(0, 2 * stages - 1, drain_stats, 0)

    def drain_weights(index, unused):
        @pl.when(section != lax.div(index, 2))
        def _():
            wait_for(weights.at[index, part], pass_send.at[index])
        return 0

    lax.fori_loop(0, 2 * blocks, drain_weights, 0)

    def drain_grads(k, unused):
        wait_for(core_part.at[k], grad_send.at[0, k])
        wait_for(section_part.at[k, pl.ds(0, sections - 1)], grad_send.at[1, k])
        wait_for(whole.at[k, :, 0, 0, pl.ds(0, 16 * (chips - 1)), pl.ds(0, half)], grad_send.at[2, k])
        if groups > 1:
            wait_for(group_part.at[k, pl.ds(0, groups - 1)], group_send.at[k])

        @pl.when((k > 0) & (section != block_of(k)))
        def _():
            wait_for(whole.at[k, :, :, 0, pl.ds(0, 16)], grad_send.at[3, k])

        @pl.when((k > 0) & (section == block_of(k)))
        def _():
            wait_for(whole.at[k, :, :, 0], grad_send.at[4, k])
        return 0

    lax.fori_loop(0, stages, drain_grads, 0)
    wait_for(whole.at[0, :, :, 0, pl.ds(0, 16 * (sections - 1))], grad_send.at[3, 0])
    wait_for(whole.at[0, :, :, 0], grad_send.at[4, 0])
    wait_for(flat_core, grad_send.at[0, extra])
    wait_for(flat_section.at[pl.ds(0, sections - 1)], grad_send.at[1, extra])
    wait_for(flat_whole.at[0, 0, pl.ds(0, 48 * (chips - 1)), pl.ds(0, half)], grad_send.at[2, extra])
    wait_for(flat_whole.at[:, 0, pl.ds(0, 48 * (sections - 1))], grad_send.at[3, extra])
    wait_for(flat_whole.at[:, 0], grad_send.at[4, extra])
    if groups > 1:
        wait_for(flat_group.at[0, pl.ds(0, groups - 1)], group_send.at[extra])
    first_copy.wait()
    second_copy.wait()
    unite_done.wait()
    camera_done.wait()


def body(
    lidar, context, depth_logits, cell_index, unite_weight, unite_gain, unite_bias, first_weight, second_weight,
    first_gain, first_bias, second_gain, second_bias, cotangent,
):
    peers = lax.axis_size("dp")
    sections = lax.axis_size("section")
    section = lax.axis_index("section")
    channels = cotangent.shape[-1]
    pixels, bins = depth_logits.shape[2:]
    cam = context.shape[-1]
    united_in = unite_weight.shape[1]
    blocks = sections
    stages = 2 * blocks + 1
    events = 2 * stages - 1
    groups = peers // (2 * chips)
    taken = 9 * channels

    vmem = pl.BlockSpec(memory_space=pltpu.VMEM)
    hbm = pl.BlockSpec(memory_space=pl.ANY)
    shape = jax.ShapeDtypeStruct
    dma = pltpu.SemaphoreType.DMA
    act, lidar_grad, context_grad, logit_grad, unite_grad, camera_grad, first_grad, second_grad, sums = pl.pallas_call(
        functools.partial(kernel, peers, sections),
        out_shape=(
            shape((cells, channels), f32),
            shape((cells, channels), f32),
            shape((pixels, cam), f32),
            shape((pixels, bins), f32),
            shape((9, 2, 2, 64, channels), bf16),
            shape((2, 2, flat_rows // 4, channels), bf16),
            shape((9, 2, 2, 64, channels), bf16),
            shape((9, 2, 2, 64, channels), bf16),
            shape((stages, 2, channels), f32),
        ),
        in_specs=[hbm, vmem, vmem, vmem, hbm, vmem, vmem, hbm, hbm, vmem, vmem, vmem, vmem, hbm],
        out_specs=[vmem, vmem, vmem, vmem, hbm, hbm, hbm, hbm, vmem],
        scratch_shapes=[
            pltpu.VMEM((2 * blocks, taken, channels), bf16),
            pltpu.VMEM((9 * united_in, channels), bf16),
            pltpu.VMEM((blocks, 4, channels), f32),
            pltpu.VMEM((cells + 2 * side, 3 * wide), bf16),
            pltpu.VMEM((chips, cells + 2 * side, 3 * channels), bf16),
            pltpu.VMEM((chips, cells, channels), bf16),
            pltpu.VMEM((2 * blocks, chips, cells, channels), bf16),
            pltpu.VMEM((stages, chips, cells, channels), f32),
            pltpu.VMEM((stages + 1, 1, channels), f32),
            pltpu.VMEM((chips, cells, channels), f32),
            pltpu.VMEM((chips, cells, channels), bf16),
            pltpu.VMEM((chips, cells, channels), bf16),
            pltpu.VMEM((chips, cells, channels), bf16),
            pltpu.VMEM((chips, cells, half), bf16),
            pltpu.VMEM((events, 2, channels), f32),
            pltpu.VMEM((events, 2 * groups, 2, channels), f32),
            pltpu.VMEM((2, channels), f32),
            pltpu.VMEM((peers, 2, channels), f32),
            pltpu.VMEM((pixels, half), f32),
            pltpu.VMEM((pixels, half), jnp.int32),
            pltpu.VMEM((2, half, pixels), f32),
            pltpu.VMEM((cells, pixels), bf16),
            pltpu.VMEM((stages, 9, 2, 64, half), bf16),
            pltpu.VMEM((stages, 9, 64, half), bf16),
            pltpu.VMEM((stages, 9, 64, half), bf16),
            pltpu.VMEM((stages, sections, 9, 16, half), bf16),
            pltpu.VMEM((stages, 9, 2, 2, 64, channels), bf16),
            pltpu.VMEM((flat_rows, half), bf16),
            pltpu.VMEM((flat_rows // 4, half), bf16),
            pltpu.VMEM((flat_rows // 4, half), bf16),
            pltpu.VMEM((sections, 48, half), bf16),
            pltpu.VMEM((2, 2, flat_rows // 4, channels), bf16),
            pltpu.VMEM((sections, stages, 2, channels), f32),
            pltpu.VMEM((stages if groups > 1 else 1, groups, 9, 16, half), bf16),
            pltpu.VMEM((1, groups, 48, half), bf16),
            dma((9,)), dma, dma, dma((events,)), dma((events,)), dma((chips,)), dma((chips,)), dma((chips,)),
            dma((chips,)), dma((chips,)), dma((chips,)), dma((chips,)), dma((chips,)), dma((4,)),
            dma((2 * blocks,)), dma((2,)), dma((2 * blocks,)), dma((2 * blocks,)), dma, dma,
            dma((5, stages + 1)), dma((5, stages + 1)), dma, dma, dma((stages + 1,)), dma((stages + 1,)),
        ],
        compiler_params=pltpu.CompilerParams(
            collective_id=0, has_side_effects=True, vmem_limit_bytes=56 << 20
        ),
    )(
        lidar.reshape(cells, channels), context.reshape(pixels, cam), depth_logits.reshape(pixels, bins),
        cell_index.reshape(pixels, bins), unite_weight.reshape(-1, channels),
        unite_gain[None], unite_bias[None], first_weight.reshape(taken, channels),
        second_weight.reshape(taken, channels), first_gain, first_bias, second_gain, second_bias,
        cotangent.reshape(-1, cells, channels),
    )

    camera_rows = camera_grad.reshape(-1, channels)[: 9 * cam].reshape(9, cam, channels)
    unite_whole = jnp.concatenate(
        [unite_grad.reshape(9, channels, channels).astype(f32), camera_rows.astype(f32)], axis=1
    )
    own = lax.dynamic_slice_in_dim(sums[1:].reshape(blocks, 2, 2, channels), section, 1, 0)
    return (
        act.reshape(lidar.shape),
        lidar_grad.reshape(lidar.shape),
        context_grad.reshape(context.shape),
        logit_grad.reshape(depth_logits.shape),
        unite_whole,
        sums[0, 1],
        sums[0, 0],
        first_grad.reshape(first_weight.shape).astype(f32),
        second_grad.reshape(second_weight.shape).astype(f32),
        own[:, 0, 1],
        own[:, 0, 0],
        own[:, 1, 1],
        own[:, 1, 0],
    )


def solution(mesh):
    split, by_dp = P("section"), P("section", "dp")
    in_specs = (by_dp, by_dp, by_dp, by_dp, P(), P(), P(), split, split, split, split, split, split, P(None, "dp"))
    out_specs = (by_dp, by_dp, by_dp, by_dp, P(), P(), P(), split, split, split, split, split, split)
    return jax.shard_map(body, mesh=mesh, in_specs=in_specs, out_specs=out_specs, check_vma=False)
```

time: 553 us -> 173 us (0.31)
  waiting for transfers between devices: 305 us -> 0 us
  blocking collectives: 110 us -> 0 us
  Pallas kernels: 96.9 us -> 153 us
  between operations: 13.9 us -> 0.68 us
  other arithmetic: 13.9 us -> 6.56 us
    unnamed x7 -> x0, waiting for transfers between devices: 185 us -> none
    all_gather x2 -> x0, waiting for transfers between devices: 106 us -> none  [gathered(): return lax.all_gather(array, 'section', axis=0, tiled=True)]
    psum x2 -> x0, blocking collectives: 100 us -> none  [the longest x1 84.7 us: body(): whole = lax.psum(unite_grad.astype(f32), ('section', 'dp'))]
    pallas_call x1, Pallas kernels: 96.9 us -> 153 us  [body(): pl.pallas_call(functools.partial(kernel, peers, sections), out_shape=(sha...]
    psum x1 -> x0, waiting for transfers between devices: 13.8 us -> none  [body(): lax.psum(lax.psum_scatter(first_grad.astype(f32), 'section', scatter_dime...]
    convert_element_type x2, other arithmetic: 13.9 us -> 3.26 us  [the longest x1 1.63 us: body(): first_grad.reshape(first_weight.shape).astype(f32)]
    all_gather x1 -> x0, blocking collectives: 9.62 us -> none  [gathered(): return lax.all_gather(array, 'section', axis=0, tiled=True)]
  transfers between devices with their start and end apart: 5 -> 0, of which waited for: 5 -> 0; matrix products, arithmetic and copies ran while one was open for 2% -> 0% of each run, Pallas kernels for 0% -> 0%
where the time goes in v2:
time: 173 us; the launch traced here: 172 us
  Pallas kernels  153 us (88%)
  local copies, waits for them, and re-layouts  12.6 us (7%)
  other arithmetic  6.56 us (4%)
    pallas_call x1, Pallas kernels, body(): pl.pallas_call(functools.partial(kernel, peers, sections), out_shape=(sha...  153 us
    unnamed x15, local copies, waits for them, and re-layouts  9 us

profile of v2, /device:TPU:0, one launch (start us, length us, event | category | flops | bytes accessed | tf_op | source)
XLA Modules:
  0.0 172.4 jit_solution(8292466671106709813)
XLA Ops:
  0.6 1.4 copy.27
  2.1 1.5 copy.28
  3.6 1.6 copy.29
  5.1 152.6 %shard_map.237 = (f32[256,256]{1,0:T(8,128)}, f32[256,256]{1,0:T(8,128)}, f32[128,80]{1,0:T(8,128)}, f32[128,118]{1,0:T(8,128)}, bf16[9,2,2,64,256]{4,3,2,1,0:T(...) custom-call(bf16[256,256]{1,0:T(8,128)(2,1)} %bitcast.46, ...), custom_call_target="tpu_custom_call" | custom-call | tf_op jit(solution)/shard_map/pallas_call | solution.py:786
  157.7 1.3 fusion
  159.0 0.7 slice.27
  159.7 0.6 dynamic-slice_bitcast_fusion
  160.3 1.5 copy.30
  161.9 1.6 copy.31
  163.4 1.0 slice.32
  164.4 0.0 copy-start.1
  164.5 3.3 %maximum_convert_fusion = f32[9,336,256]{2,1,0:T(8,128)} fusion(bf16[9,80,256]{2,1,0:T(8,128)(2,1)S(1)} %bitcast.33, bf16[9,256,256]{2,1,0:T(8,128)(2,1)} %bitcast.38), kind=kLoop, calls=%fused_computation | loop fusion | flops 3096576 | bytes 4644864 | tf_op jit(solution)/shard_map/concatenate | solution.py:854
  167.8 0.0 copy-done.1
  167.8 0.0 copy-start
  167.8 1.6 convert.5
  169.4 0.0 copy-done
  169.4 0.0 copy-start.3
  169.4 0.0 copy-start.2
  169.4 1.6 convert.6
  171.0 0.0 copy-done.3
  171.0 0.7 copy.34
  171.7 0.0 copy-done.2
  171.7 0.7 copy.35
Async XLA Ops:
  164.4 3.3 %copy-start.1 = (bf16[9,2,2,64,256]{4,3,2,1,0:T(8,128)(2,1)S(1)}, bf16[9,2,2,64,256]{4,3,2,1,0:T(8,128)(2,1)}, u32[]{:S(2)}) copy-start(bf16[9,2,2,64,256]{4,3,2,1,0:T(8,128)(2,1)} %get-tuple-element.29) | copy-start | bytes 3538948
  167.8 1.6 copy-start
  169.4 1.6 copy-start.3
  169.4 2.3 %copy-start.2 = (f32[256,256]{1,0:T(8,128)S(1)}, f32[256,256]{1,0:T(8,128)}, u32[]{:S(2)}) copy-start(f32[256,256]{1,0:T(8,128)} %get-tuple-element.23) | copy-start | bytes 786436

commit v3 on v2

--- a/solution.py
+++ b/solution.py
@@ -69,13 +69,32 @@
     )
 
 
+plan = {
+    "start": [("offer", 0, "near", 0), ("offer", 1, "near", 3), ("offer", 1, "near", 1), ("offer", 1, "near", 2), ("offer", 0, "near", 1)],
+    "lift1": [("offer", 1, "near", 0), ("offer", 0, "near", 2)],
+    "lift2": [("offer", 0, "far", 0)],
+    "united": [("relay", 0, 0), ("offer", 1, "far", 2), ("offer", 1, "far", 0), ("relay", 2, 1)],
+    "united2": [("relay", 0, 1), ("offer", 0, "far", 1)],
+    "merged": [("offer", 1, "far", 1), ("offer", 0, "near", 3), ("offer", 0, "far", 2), ("relay", 1, 0)],
+    "entered1": [("relay", 1, 1), ("relay", 3, 0)],
+    "entered3": [("relay", 2, 0), ("arrive", 0, 0), ("offer", 0, "far", 3)],
+    "entered2": [("arrive", 2, 1)],
+    "entered": [("relay", 3, 1)],
+    ("first", 0): [("arrive", 0, 1)],
+    ("second", 0): [("offer", 1, "far", 3), ("arrive", 1, 0)],
+    ("first", 1): [("arrive", 2, 0), ("arrive", 1, 1)],
+    ("first", 2): [("arrive", 3, 0)],
+    ("first", 3): [("arrive", 3, 1)],
+}
+
+
 def kernel(
     peers, sections,
     lidar_ref, context_ref, logit_ref, cell_ref, unite_ref, unite_gain, unite_bias, first_ref, second_ref,
     first_gain, first_bias, second_gain, second_bias, cotangent_ref,
-    act_ref, lidar_grad, context_grad, logit_grad, unite_out, camera_out, first_out, second_out, sums_out,
+    act_ref, lidar_grad, context_grad, logit_grad, unite_out, camera_out, first_out, second_out, small_out,
     weights, unite_weight, vectors, joined, shifted, current, kept, normed, scales, held, gathered, upstream,
-    lidars, cameras, mine, slots, unite_mine, unite_slots, probability, cell_wide, turned, histogram,
+    lidars, cameras, mine, slots, unite_mine, unite_slots, probability, places, histogram,
     partial, core_part, own_part, section_part, whole, flat, flat_core, flat_own, flat_section, flat_whole,
     totals, group_part, flat_group,
     local_sem, unite_send, unite_recv, stat_send, stat_recv, raw_send, raw_recv, cot_send, cot_recv,
@@ -91,8 +110,8 @@
     blocks = sections
     stages = 2 * blocks + 1
     channels = vectors.shape[-1]
-    bins = logit_ref.shape[1]
-    cam = context_ref.shape[1]
+    bins = logit_ref.shape[0]
+    cam = context_ref.shape[0]
     united_in = channels + cam
     taken = 9 * channels
     row_half = lax.div(chip, 2)
@@ -141,7 +160,7 @@
         vectors[section, number : number + 1] = part[...]
     joined[...] = jnp.zeros_like(joined)
     probability[...] = jnp.zeros_like(probability)
-    cell_wide[...] = jnp.zeros_like(cell_wide)
+    places[...] = jnp.zeros_like(places)
     cameras[chip] = jnp.zeros((cells, half), bf16)
     pl.semaphore_wait(barrier, peers - 1 + sections - 1)
 
@@ -201,7 +220,29 @@
         def _():
             (own_second if which else own_first).wait()
 
-    offer(0, near, 0)
+    def act_on(entry):
+        name, one, two = entry[0:3]
+        if name == "relay":
+            relay(one, two)
+        elif name == "arrive":
+            arrive(one, two)
+        else:
+            @pl.when(section == entry[3])
+            def _():
+                offer(one, near if two == "near" else far, 2 * one + (two == "far"))
+
+    def point(name, block=None):
+        for key, entries in plan.items():
+            if isinstance(key, tuple) and key[0] == name:
+                @pl.when(block == key[1])
+                def _():
+                    for entry in entries:
+                        act_on(entry)
+            elif key == name:
+                for entry in entries:
+                    act_on(entry)
+
+    point("start")
     for step in range(1, sections):
         remote(
             vectors.at[section], vectors.at[section], vector_send, vector_recv,
@@ -209,19 +250,23 @@
         ).start()
 
     logits = logit_ref[...].astype(f32)
-    raised = jnp.exp(logits - jnp.max(logits, axis=-1, keepdims=True))
-    probability[:, 0:bins] = raised / jnp.sum(raised, axis=-1, keepdims=True)
-    cell_wide[:, 0:bins] = cell_ref[...]
-    turned[0] = probability[...].T
-    turned[1] = cell_wide[...].astype(f32).T
-    address = lax.broadcasted_iota(jnp.int32, (cells, half), 0).astype(f32)
+    raised = jnp.exp(logits - jnp.max(logits, axis=0, keepdims=True))
+    probability[0:bins] = raised / jnp.sum(raised, axis=0, keepdims=True)
+    address = lax.broadcasted_iota(jnp.int32, (cells, half), 0)
 
     def add_bin(number, total):
-        return total + jnp.where(turned[1, pl.ds(number, 1)] == address, turned[0, pl.ds(number, 1)], 0.0)
-
-    counted = lax.fori_loop(0, bins, add_bin, jnp.zeros((cells, half), f32)).astype(bf16)
+        place = cell_ref[number]
+        places[pl.ds(number, 1)] = place.astype(f32)
+        return total + jnp.where(place == address, probability[pl.ds(number, 1)], 0.0)
+
+    counted = jnp.zeros((cells, half), f32)
+    for number in range(3):
+        counted = lax.fori_loop(bins * number // 3, bins * (number + 1) // 3, add_bin, counted)
+        if number < 2:
+            point(f"lift{number + 1}")
+    counted = counted.astype(bf16)
     histogram[...] = counted
-    pooled = jnp.dot(counted, context_ref[...], preferred_element_type=f32)
+    pooled = lax.dot_general(counted, context_ref[...], transposed_rhs, preferred_element_type=f32)
     cameras[chip, :, 0:cam] = pooled.astype(bf16)
 
     own_lidar.wait()
@@ -256,11 +301,7 @@
 
     lax.fori_loop(1, peers, send_unite, 0)
 
-    @pl.when(section == 0)
-    def _():
-        offer(0, far, 1)
-        offer(1, near, 2)
-
+    point("united")
     shifted[...] = jnp.zeros_like(shifted)
     flat[9 * cam :, :] = jnp.zeros((flat_rows - 9 * cam, half), bf16)
 
@@ -271,15 +312,12 @@
         square = jnp.sum(squares, axis=0, keepdims=True) + each * jnp.sum(apart * apart, axis=0, keepdims=True)
         return center, square
 
+    point("united2")
     wait_for(unite_slots.at[pl.ds(0, peers - 1)], unite_recv)
     center, square = merged(unite_slots[:, 0, :], unite_slots[:, 1, :], cells)
     scales[0] = lax.rsqrt(square * (1.0 / count) + eps)
     scales[stages] = center
-    relay(0, 0)
-
-    @pl.when(section != 0)
-    def _():
-        offer(0, far, 1)
+    point("merged")
 
     def enter(number):
         value = (gathered[number].astype(f32) - scales[stages]) * scales[0]
@@ -293,12 +331,7 @@
     for step in (1, 3, 2):
         wait_for(gathered.at[0], raw_recv.at[step])
         enter(lax.rem(chip - step + chips, chips))
-        if step == 1:
-            relay(1, 0)
-
-            @pl.when(section == 0)
-            def _():
-                offer(1, far, 3)
+        point(f"entered{step}")
 
     own_cot.wait()
     for step in range(1, chips):
@@ -309,13 +342,7 @@
         remote(lidars.at[chip], lidars.at[chip], lidar_send.at[step], lidar_recv.at[step], peer).start()
         remote(cameras.at[chip], cameras.at[chip], camera_send.at[step], camera_recv.at[step], peer).start()
 
-    arrive(0, 0)
-    relay(0, 1)
-
-    @pl.when(section != 0)
-    def _():
-        offer(1, near, 2)
-
+    point("entered")
     wait_for(vectors.at[pl.ds(0, sections - 1)], vector_recv)
 
     members = 2 * groups
@@ -367,33 +394,10 @@
             return vectors[s, number : number + 1]
 
         def during_first():
-            @pl.when(s == 0)
-            def _():
-                relay(2, 0)
-
-                @pl.when(section != 0)
-                def _():
-                    offer(1, far, 3)
-
-            @pl.when(s == 1)
-            def _():
-                relay(2, 1)
-
-            arrive(s, 1)
+            point("first", s)
 
         def during_second():
-            @pl.when(s == 0)
-            def _():
-                relay(3, 0)
-                relay(1, 1)
-
-            @pl.when(s == 1)
-            def _():
-                relay(3, 1)
-
-            @pl.when(s < blocks - 1)
-            def _():
-                arrive(s + 1, 0)
+            point("second", s)
 
         def use_first(number, value):
             hidden = silu(vector(0) * value + vector(1))
@@ -489,7 +493,8 @@
     def column_arrived(k):
         wait_for(whole.at[k, :, 0, 0, pl.ds(0, 16 * (chips - 1)), pl.ds(0, half)], grad_recv.at[2, k])
 
-    def to_owner(k, block):
+    def to_owner(k):
+        block = block_of(k)
         column_arrived(k)
         place = whole.at[k, :, :, core, rows16]
 
@@ -509,8 +514,8 @@
         place = whole.at[k, :, :, core]
         remote(place, place, grad_send.at[4, k], grad_recv.at[4, k], at(other=sibling)).start()
 
-    def owner_share(k, block):
-        @pl.when(section == block)
+    def owner_share(k):
+        @pl.when(section == block_of(k))
         def _():
             share(k)
 
@@ -520,13 +525,10 @@
     def block_of(k):
         return lax.div(k - 1, 2)
 
-    def advance(slot):
-        due = ((2, to_sections), (4, to_column), (6, lambda k: to_owner(k, block_of(k))),
-               (8, lambda k: owner_share(k, block_of(k))))
-        for ahead, act in due:
-            @pl.when(slot + ahead <= stages - 1)
-            def _():
-                act(slot + ahead)
+    def when_due(k, act):
+        @pl.when(k <= stages - 1)
+        def _():
+            act(k)
 
     def backward_stage(stage, gain, bias, gradient, meanwhile):
         event = stages - 1 + stage
@@ -569,43 +571,43 @@
             @pl.when(back > 0)
             def _():
                 weight_grad(stage + 2, kept.at[stage + 1])
-            advance(stage + 1)
+            when_due(stage + 4, to_column)
 
         def during_first():
             weight_grad(stage + 1, kept.at[stage])
-            advance(stage)
+            when_due(stage + 3, to_column)
 
         backward_stage(stage + 1, vector(2), vector(3), lambda number: upstream[number].astype(f32), during_second)
         for number in range(chips):
             held[number] = conv_transposed(
                 shifted.at[number], lambda tap: weights[2 * s + 1, channels * tap : channels * (tap + 1), :], channels
             )
+        when_due(stage + 2, to_sections)
+        when_due(stage + 6, to_owner)
         backward_stage(stage, vector(0), vector(1), lambda number: held[number], during_first)
         for number in range(chips):
             passed = conv_transposed(
                 shifted.at[number], lambda tap: weights[2 * s, channels * tap : channels * (tap + 1), :], channels
             )
             upstream[number] = (upstream[number].astype(f32) + passed).astype(bf16)
+        when_due(stage + 1, to_sections)
+        when_due(stage + 5, to_owner)
         return 0
 
     lax.fori_loop(0, blocks, block_back, 0)
 
     def during_unite():
         weight_grad(1, kept.at[0])
-        advance(0)
+        to_column(3)
 
     backward_stage(
         0, unite_gain[...], unite_bias[...], lambda number: upstream[number].astype(f32), during_unite
     )
-    for step in range(1, sections):
-        remote(
-            totals.at[section], totals.at[section], total_send, total_recv,
-            at(other_section=lax.rem(section + step, sections)),
-        ).start()
     for step in range(1, chips):
         wait_for(lidars.at[0], lidar_recv.at[step])
         wait_for(cameras.at[0], camera_recv.at[step])
     weight_grad(0, lidars)
+    to_sections(1)
     held_cameras = [cameras[number] for number in range(chips)]
     for i in range(3):
         for j in range(3):
@@ -626,11 +628,15 @@
     remote(
         flat.at[sent_rows], flat_core, grad_send.at[0, extra], grad_recv.at[0, extra], at(other=sibling)
     ).start()
-    advance(-1)
+    to_sections(0)
+    to_column(2)
+    to_owner(5)
+    for step in range(1, sections):
+        remote(
+            totals.at[section], totals.at[section], total_send, total_recv,
+            at(other_section=lax.rem(section + step, sections)),
+        ).start()
     own = shifted.at[chip]
-    lidar_grad[...] = conv_transposed(
-        own, lambda tap: unite_weight[united_in * tap : united_in * tap + channels, :], channels
-    )
     pooled_grad = conv_transposed(
         own, lambda tap: unite_weight[united_in * tap + channels : united_in * (tap + 1), :], channels
     ).astype(bf16)
@@ -644,22 +650,31 @@
             flat_own.at[pl.ds(pl.multiple_of(other * 48, 16), 48)], flat_section.at[section],
             grad_send.at[1, extra], grad_recv.at[1, extra], at(other_section=other),
         ).start()
-    advance(-2)
-
-    context_grad[...] = lax.dot_general(histogram[...], pooled_grad, transposed_lhs, preferred_element_type=f32)
-    table = lax.dot_general(context_ref[...], pooled_grad, transposed_rhs, preferred_element_type=f32)
-    places = cell_wide[...]
-    within = lax.rem(places, half)
+    to_owner(4)
+    lidar_grad[...] = conv_transposed(
+        own, lambda tap: unite_weight[united_in * tap : united_in * tap + channels, :], channels
+    )
+    to_column(1)
+
+    context_grad[...] = lax.dot_general(pooled_grad, histogram[...], transposed_lhs, preferred_element_type=f32)
+    table = lax.dot_general(
+        context_ref[...], pooled_grad, (((0,), (1,)), ((), ())), preferred_element_type=f32
+    )
+    wanted = places[...].T.astype(jnp.int32)
+    within = lax.rem(wanted, half)
     low = jnp.take_along_axis(table[:, 0:half], within, axis=1)
     high = jnp.take_along_axis(table[:, half : 2 * half], within, axis=1)
+    chance_grad = jnp.where(wanted < half, low, high).T
     chance = probability[...]
-    chance_grad = jnp.where(places < half, low, high)
-    logits_grad = chance * (chance_grad - jnp.sum(chance_grad * chance, axis=-1, keepdims=True))
-    logit_grad[...] = logits_grad[:, 0:bins]
-
-    to_column(1)
-    to_owner(3, 1)
-    owner_share(5, 2)
+    places[...] = chance * (chance_grad - jnp.sum(chance_grad * chance, axis=0, keepdims=True))
+
+    def store_bin(number, unused):
+        logit_grad[number] = places[pl.ds(number, 1)]
+        return 0
+
+    lax.fori_loop(0, bins, store_bin, 0)
+
+    to_owner(3)
     to_column(0)
     wait_for(flat_section.at[pl.ds(0, sections - 1)], grad_recv.at[1, extra])
     piece = total_of(flat_section[number].astype(f32) for number in range(sections)).astype(bf16)
@@ -669,10 +684,8 @@
         remote(
             flat_place, flat_place, grad_send.at[2, extra], grad_recv.at[2, extra], at(other=chip_peer(step))
         ).start()
-    to_owner(2, 0)
-    owner_share(4, 1)
-    to_owner(1, 0)
-    owner_share(3, 1)
+    to_owner(2)
+    to_owner(1)
     to_all(0)
     wait_for(flat_whole.at[0, 0, pl.ds(0, 48 * (chips - 1)), pl.ds(0, half)], grad_recv.at[2, extra])
     flat_rows_place = flat_whole.at[:, core, flat48]
@@ -682,15 +695,26 @@
             flat_rows_place, flat_rows_place, grad_send.at[3, extra], grad_recv.at[3, extra],
             at(other_section=other),
         ).start()
-    owner_share(2, 0)
-    owner_share(1, 0)
+
+    def share_all(back, unused):
+        owner_share(stages - 1 - back)
+        return 0
+
+    lax.fori_loop(0, stages - 1, share_all, 0)
     share(0)
     wait_for(flat_whole.at[:, 0, pl.ds(0, 48 * (sections - 1))], grad_recv.at[3, extra])
     flat_half = flat_whole.at[:, core]
     remote(flat_half, flat_half, grad_send.at[4, extra], grad_recv.at[4, extra], at(other=sibling)).start()
 
     wait_for(totals.at[pl.ds(0, sections - 1)], total_recv)
-    sums_out[...] = total_of(totals[number] for number in range(sections))
+    def summed(stage, row):
+        return total_of(totals[number, stage, row : row + 1] for number in range(sections))
+
+    small_out[0] = summed(0, 1)
+    small_out[1] = summed(0, 0)
+    for number in range(2):
+        small_out[2 + 2 * number] = summed(2 * section + 1 + number, 1)
+        small_out[3 + 2 * number] = summed(2 * section + 1 + number, 0)
     shared(2 * section + 1)
     shared(2 * section + 2)
     first_copy = pltpu.make_async_copy(whole.at[2 * section + 1], first_out, local_sem.at[5])
@@ -760,6 +784,51 @@
     second_copy.wait()
     unite_done.wait()
     camera_done.wait()
+
+
+def widen(cam, *refs):
+    held_in, outs, narrow, full = refs[0:9], refs[9:22], refs[22:31], refs[31:34]
+    in_sem, out_sem, plain_sem = refs[34:37]
+    loads = [pltpu.make_async_copy(a, b, in_sem.at[n]) for n, (a, b) in enumerate(zip(held_in, narrow))]
+    for load in loads:
+        load.start()
+    passed = []
+    channels = full[1].shape[-1]
+
+    def store(number, tap):
+        return pltpu.make_async_copy(full[number].at[tap], outs[10 + number].at[tap], out_sem.at[number, tap])
+
+    loads[0].wait()
+    loads[1].wait()
+
+    def unite_tap(tap, unused):
+        full[0][tap, 0:channels] = narrow[0][tap].astype(f32)
+        rows = pl.ds(pl.multiple_of(cam * tap, 16), cam)
+        full[0][tap, channels : channels + cam] = narrow[1][rows].astype(f32)
+        store(0, tap).start()
+        return 0
+
+    lax.fori_loop(0, 9, unite_tap, 0)
+    for number in (1, 2):
+        loads[number + 1].wait()
+
+        def block_tap(tap, unused):
+            full[number][tap] = narrow[number + 1][tap].astype(f32)
+            store(number, tap).start()
+            return 0
+
+        lax.fori_loop(0, 9, block_tap, 0)
+    for number in range(4, 9):
+        loads[number].wait()
+    for number in range(10):
+        source = narrow[4 + number] if number < 4 else narrow[8].at[number - 4]
+        passed.append(pltpu.make_async_copy(source, outs[number], plain_sem.at[number]))
+        passed[-1].start()
+    for number in range(3):
+        for tap in range(9):
+            store(number, tap).wait()
+    for copy in passed:
+        copy.wait()
 
 
 def body(
@@ -780,21 +849,21 @@
     taken = 9 * channels
 
     vmem = pl.BlockSpec(memory_space=pltpu.VMEM)
-    hbm = pl.BlockSpec(memory_space=pl.ANY)
+    hbm = pl.BlockSpec(memory_space=pltpu.HBM)
     shape = jax.ShapeDtypeStruct
     dma = pltpu.SemaphoreType.DMA
-    act, lidar_grad, context_grad, logit_grad, unite_grad, camera_grad, first_grad, second_grad, sums = pl.pallas_call(
+    results = pl.pallas_call(
         functools.partial(kernel, peers, sections),
         out_shape=(
             shape((cells, channels), f32),
             shape((cells, channels), f32),
-            shape((pixels, cam), f32),
-            shape((pixels, bins), f32),
+            shape((cam, pixels), f32),
+            shape((bins, 1, pixels), f32),
             shape((9, 2, 2, 64, channels), bf16),
             shape((2, 2, flat_rows // 4, channels), bf16),
             shape((9, 2, 2, 64, channels), bf16),
             shape((9, 2, 2, 64, channels), bf16),
-            shape((stages, 2, channels), f32),
+            shape((6, 1, channels), f32),
         ),
         in_specs=[hbm, vmem, vmem, vmem, hbm, vmem, vmem, hbm, hbm, vmem, vmem, vmem, vmem, hbm],
         out_specs=[vmem, vmem, vmem, vmem, hbm, hbm, hbm, hbm, vmem],
@@ -817,9 +886,8 @@
             pltpu.VMEM((events, 2 * groups, 2, channels), f32),
             pltpu.VMEM((2, channels), f32),
             pltpu.VMEM((peers, 2, channels), f32),
-            pltpu.VMEM((pixels, half), f32),
-            pltpu.VMEM((pixels, half), jnp.int32),
-            pltpu.VMEM((2, half, pixels), f32),
+            pltpu.VMEM((half, pixels), f32),
+            pltpu.VMEM((half, pixels), f32),
             pltpu.VMEM((cells, pixels), bf16),
             pltpu.VMEM((stages, 9, 2, 64, half), bf16),
             pltpu.VMEM((stages, 9, 64, half), bf16),
@@ -843,32 +911,58 @@
             collective_id=0, has_side_effects=True, vmem_limit_bytes=56 << 20
         ),
     )(
-        lidar.reshape(cells, channels), context.reshape(pixels, cam), depth_logits.reshape(pixels, bins),
-        cell_index.reshape(pixels, bins), unite_weight.reshape(-1, channels),
+        lidar.reshape(cells, channels), context.reshape(pixels, cam).T, depth_logits.reshape(pixels, bins).T,
+        jnp.transpose(cell_index, (0, 3, 1, 2)).reshape(bins, 1, pixels), unite_weight.reshape(-1, channels),
         unite_gain[None], unite_bias[None], first_weight.reshape(taken, channels),
         second_weight.reshape(taken, channels), first_gain, first_bias, second_gain, second_bias,
         cotangent.reshape(-1, cells, channels),
     )
 
-    camera_rows = camera_grad.reshape(-1, channels)[: 9 * cam].reshape(9, cam, channels)
-    unite_whole = jnp.concatenate(
-        [unite_grad.reshape(9, channels, channels).astype(f32), camera_rows.astype(f32)], axis=1
+    act, lidar_grad, context_grad, logit_grad, *small, unite_whole, first_whole, second_whole = pl.pallas_call(
+        functools.partial(widen, cam),
+        out_shape=(
+            shape((cells, channels), f32),
+            shape((cells, channels), f32),
+            shape((cam, pixels), f32),
+            shape((bins, 1, pixels), f32),
+            *[shape((1, channels), f32)] * 6,
+            shape((9, united_in, channels), f32),
+            shape((9, channels, channels), f32),
+            shape((9, channels, channels), f32),
+        ),
+        in_specs=[hbm] * 9,
+        out_specs=[hbm] * 13,
+        scratch_shapes=[
+            pltpu.VMEM((9, channels, channels), bf16),
+            pltpu.VMEM((flat_rows, channels), bf16),
+            pltpu.VMEM((9, channels, channels), bf16),
+            pltpu.VMEM((9, channels, channels), bf16),
+            pltpu.VMEM((cells, channels), f32),
+            pltpu.VMEM((cells, channels), f32),
+            pltpu.VMEM((cam, pixels), f32),
+            pltpu.VMEM((bins, 1, pixels), f32),
+            pltpu.VMEM((6, 1, channels), f32),
+            pltpu.VMEM((9, united_in, channels), f32),
+            pltpu.VMEM((9, channels, channels), f32),
+            pltpu.VMEM((9, channels, channels), f32),
+            dma((9,)), dma((3, 9)), dma((10,)),
+        ],
+        compiler_params=pltpu.CompilerParams(vmem_limit_bytes=60 << 20),
+    )(
+        results[4].reshape(9, channels, channels), results[5].reshape(flat_rows, channels),
+        results[6].reshape(9, channels, channels), results[7].reshape(9, channels, channels), *results[0:4], results[8],
     )
-    own = lax.dynamic_slice_in_dim(sums[1:].reshape(blocks, 2, 2, channels), section, 1, 0)
     return (
         act.reshape(lidar.shape),
         lidar_grad.reshape(lidar.shape),
-        context_grad.reshape(context.shape),
-        logit_grad.reshape(depth_logits.shape),
+        context_grad.T.reshape(context.shape),
+        jnp.transpose(logit_grad.reshape(1, bins, 1, pixels), (0, 2, 3, 1)),
         unite_whole,
-        sums[0, 1],
-        sums[0, 0],
-        first_grad.reshape(first_weight.shape).astype(f32),
-        second_grad.reshape(second_weight.shape).astype(f32),
-        own[:, 0, 1],
-        own[:, 0, 0],
-        own[:, 1, 1],
-        own[:, 1, 0],
+        small[0].reshape(channels),
+        small[1].reshape(channels),
+        first_whole.reshape(first_weight.shape),
+        second_whole.reshape(second_weight.shape),
+        *small[2:6],
     )
 
 

time: 173 us -> 149 us (0.86)
  local copies, waits for them, and re-layouts: 12.6 us -> 0 us
  other arithmetic: 6.56 us -> 0 us
  Pallas kernels: 153 us -> 148 us
    pallas_call x1, Pallas kernels: 153 us -> 143 us  [body(): pl.pallas_call(functools.partial(kernel, peers, sections), out_shape=(sha...]
    unnamed x15 -> x0, local copies, waits for them, and re-layouts: 9 us -> none
    pallas_call x0 -> x1, Pallas kernels: none -> 5.06 us  [body(): pl.pallas_call(functools.partial(widen, cam), out_shape=(shape((cells, ch...]
    concatenate x1 -> x0, other arithmetic: 3.31 us -> none  [body(): jnp.concatenate([unite_grad.reshape(9, channels, channels).astype(f32), c...]
    convert_element_type x2 -> x0, other arithmetic: 3.26 us -> none  [the longest x1 1.63 us: body(): first_grad.reshape(first_weight.shape).astype(f32)]
    slice x3 -> x0, local copies, waits for them, and re-layouts: 3.06 us -> none  [the longest x1 1.33 us: body(): sums[0, 0]]
where the time goes in v3:
time: 149 us
  Pallas kernels  148 us (99%)
    pallas_call x1, Pallas kernels, body(): pl.pallas_call(functools.partial(kernel, peers, sections), out_shape=(sha...  143 us
    pallas_call x1, Pallas kernels, body(): pl.pallas_call(functools.partial(widen, cam), out_shape=(shape((cells, ch...  5.06 us

profile of v3, /device:TPU:0, one launch (start us, length us, event | category | flops | bytes accessed | tf_op | source)
XLA Modules:
  0.0 149.1 jit_solution(3908596370742324555)
XLA Ops:
  0.7 143.2 %shard_map.237 = (f32[256,256]{1,0:T(8,128)}, f32[256,256]{1,0:T(8,128)}, f32[80,128]{1,0:T(8,128)}, f32[118,1,128]{2,1,0:T(1,128)}, bf16[9,2,2,64,256]{4,3,2,1,...) custom-call(bf16[256,256]{1,0:T(8,128)(2,1)} %bitcast.40, ...), custom_call_target="tpu_custom_call" | custom-call | tf_op jit(solution)/shard_map/pallas_call | solution.py:855
  143.9 5.1 %shard_map.238 = (f32[256,256]{1,0:T(8,128)}, f32[256,256]{1,0:T(8,128)}, f32[80,128]{1,0:T(8,128)}, f32[118,1,128]{2,1,0:T(1,128)}, f32[1,256]{1,0:T(1,128)}, /...) custom-call(bf16[9,256,256]{2,1,0:T(8,128)(2,1)} %bitcast.35, ...), custom_call_target="tpu_custom_call" | custom-call | tf_op jit(solution)/shard_map/pallas_call | solution.py:921

commit v4 on v3

--- a/solution.py
+++ b/solution.py
@@ -70,21 +70,20 @@
 
 
 plan = {
-    "start": [("offer", 0, "near", 0), ("offer", 1, "near", 3), ("offer", 1, "near", 1), ("offer", 1, "near", 2), ("offer", 0, "near", 1)],
-    "lift1": [("offer", 1, "near", 0), ("offer", 0, "near", 2)],
-    "lift2": [("offer", 0, "far", 0)],
-    "united": [("relay", 0, 0), ("offer", 1, "far", 2), ("offer", 1, "far", 0), ("relay", 2, 1)],
-    "united2": [("relay", 0, 1), ("offer", 0, "far", 1)],
-    "merged": [("offer", 1, "far", 1), ("offer", 0, "near", 3), ("offer", 0, "far", 2), ("relay", 1, 0)],
-    "entered1": [("relay", 1, 1), ("relay", 3, 0)],
-    "entered3": [("relay", 2, 0), ("arrive", 0, 0), ("offer", 0, "far", 3)],
-    "entered2": [("arrive", 2, 1)],
-    "entered": [("relay", 3, 1)],
-    ("first", 0): [("arrive", 0, 1)],
-    ("second", 0): [("offer", 1, "far", 3), ("arrive", 1, 0)],
-    ("first", 1): [("arrive", 2, 0), ("arrive", 1, 1)],
-    ("first", 2): [("arrive", 3, 0)],
-    ("first", 3): [("arrive", 3, 1)],
+    "start": [("offer", 0, "near", 0), ("offer", 0, "far", 3), ("offer", 0, "near", 2), ("offer", 0, "near", 1)],
+    "lift2": [("offer", 0, "near", 3), ("offer", 1, "near", 0)],
+    "united": [("relay", 0, 0), ("offer", 1, "near", 1), ("offer", 1, "near", 3)],
+    "united2": [("offer", 1, "far", 0), ("offer", 1, "near", 2), ("offer", 0, "far", 1)],
+    "merged": [("offer", 0, "far", 0), ("relay", 1, 0)],
+    "entered1": [("relay", 3, 0), ("relay", 0, 1), ("relay", 2, 0)],
+    "entered3": [("offer", 0, "far", 2), ("offer", 1, "far", 1)],
+    "entered2": [("relay", 2, 1)],
+    "entered": [("offer", 1, "far", 2), ("arrive", 0, 0)],
+    ("first", 0): [("relay", 1, 1), ("arrive", 1, 0), ("offer", 1, "far", 3), ("arrive", 0, 1)],
+    ("second", 0): [("relay", 3, 1)],
+    ("first", 1): [("arrive", 1, 1), ("arrive", 2, 0)],
+    ("second", 1): [("arrive", 3, 0), ("arrive", 2, 1)],
+    ("second", 2): [("arrive", 3, 1)],
 }
 
 
@@ -428,7 +427,6 @@
     lax.fori_loop(0, blocks, block, 0)
     act_ref[...] = held[chip]
 
-    rows16 = pl.ds(pl.multiple_of(section * 16, 16), 16)
     lanes = pl.ds(pl.multiple_of(lane_half * half, half), half)
     flat48 = pl.ds(pl.multiple_of(section * 48, 16), 48)
 
@@ -458,53 +456,121 @@
             partial.at[k, :, 1 - core], core_part.at[k], grad_send.at[0, k], grad_recv.at[0, k], at(other=sibling)
         ).start()
 
-    def to_sections(k):
+    def block_of(k):
+        return lax.div(k - 1, 2)
+
+    def roles(k):
+        block = block_of(k)
+        across_x = block + 1 - 2 * lax.rem(block, 2)
+        across_y = lax.rem(block + 2, sections)
+        return block, sections - 1 - block, across_x + core * (across_y - across_x)
+
+    def tile(index):
+        return pl.ds(pl.multiple_of(index * 16, 16), 16)
+
+    def sum_cores(k):
         wait_for(core_part.at[k], grad_recv.at[0, k])
         for tap in range(9):
             own_part[k, tap] = (partial[k, tap, core].astype(f32) + core_part[k, tap].astype(f32)).astype(bf16)
-        section_part[k, section] = own_part[k, :, rows16]
+
+    def send_tile(k, index, slot, other):
+        remote(
+            own_part.at[k, :, tile(index)], section_part.at[k, slot, section], grad_send.at[1, k], grad_recv.at[1, k],
+            at(other_section=other),
+        ).start()
+
+    def to_sections(k):
+        sum_cores(k)
+        block, diagonal, helper = roles(k)
         for step in range(1, sections):
             other = lax.rem(section + step, sections)
-            remote(
-                own_part.at[k, :, pl.ds(pl.multiple_of(other * 16, 16), 16)], section_part.at[k, section],
-                grad_send.at[1, k], grad_recv.at[1, k], at(other_section=other),
-            ).start()
-
-    def over_groups(k, value, buffer, number):
+
+            @pl.when(other != diagonal)
+            def _():
+                send_tile(k, other, 0, other)
+
+            @pl.when(other == helper)
+            def _():
+                send_tile(k, diagonal, 1, other)
+
+        section_part[k, 0, section] = own_part[k, :, tile(section)]
+
+        @pl.when(section == helper)
+        def _():
+            section_part[k, 1, section] = own_part[k, :, tile(diagonal)]
+
+    def over_groups(slot, k, value, buffer, number):
         if groups == 1:
             return value
-        buffer[k, group] = value
+        mine_here = buffer.at[k, slot, group]
+        mine_here[...] = value
         for step in range(1, groups):
             to = lax.rem(group + step, groups) * (2 * chips) + chip * 2 + core
             remote(
-                buffer.at[k, group], buffer.at[k, group], group_send.at[number], group_recv.at[number], at(other=to)
+                mine_here, mine_here, group_send.at[slot, number], group_recv.at[slot, number], at(other=to)
             ).start()
-        wait_for(buffer.at[k, pl.ds(0, groups - 1)], group_recv.at[number])
-        return jnp.sum(buffer[k].astype(f32), axis=0).astype(bf16)
-
-    def to_column(k):
-        wait_for(section_part.at[k, pl.ds(0, sections - 1)], grad_recv.at[1, k])
-        piece = total_of(section_part[k, number].astype(f32) for number in range(sections)).astype(bf16)
-        place = whole.at[k, :, row_half, core, rows16, lanes]
-        place[...] = over_groups(k, piece, group_part, k)
+        wait_for(buffer.at[k, slot, pl.ds(0, groups - 1)], group_recv.at[slot, number])
+        return jnp.sum(buffer[k, slot].astype(f32), axis=0).astype(bf16)
+
+    def reduce_tile(k, slot, index):
+        piece = total_of(section_part[k, slot, number].astype(f32) for number in range(sections)).astype(bf16)
+        place = whole.at[k, :, row_half, core, tile(index), lanes]
+        place[...] = over_groups(slot, k, piece, group_part, k)
         for step in range(1, chips):
             remote(place, place, grad_send.at[2, k], grad_recv.at[2, k], at(other=chip_peer(step))).start()
 
-    def column_arrived(k):
-        wait_for(whole.at[k, :, 0, 0, pl.ds(0, 16 * (chips - 1)), pl.ds(0, half)], grad_recv.at[2, k])
+    def to_column(k):
+        block, diagonal, helper = roles(k)
+
+        @pl.when(section == helper)
+        def _():
+            wait_for(section_part.at[k, :, pl.ds(0, sections - 1)], grad_recv.at[1, k])
+            reduce_tile(k, 0, section)
+            reduce_tile(k, 1, diagonal)
+
+        @pl.when((section != helper) & (section != diagonal))
+        def _():
+            wait_for(section_part.at[k, 0, pl.ds(0, sections - 1)], grad_recv.at[1, k])
+            reduce_tile(k, 0, section)
+
+    def column_part(k, tiles):
+        return whole.at[k, :, 0, 0, pl.ds(0, 16 * (chips - 1)), pl.ds(0, half * tiles)]
+
+    def hand_over(k, index, block):
+        place = whole.at[k, :, :, core, tile(index)]
+        remote(place, place, grad_send.at[3, k], grad_recv.at[3, k], at(other_section=block)).start()
 
     def to_owner(k):
-        block = block_of(k)
-        column_arrived(k)
-        place = whole.at[k, :, :, core, rows16]
-
-        @pl.when(section != block)
-        def _():
-            remote(place, place, grad_send.at[3, k], grad_recv.at[3, k], at(other_section=block)).start()
+        block, diagonal, helper = roles(k)
+
+        @pl.when(section == helper)
+        def _():
+            wait_for(column_part(k, 2), grad_recv.at[2, k])
+            hand_over(k, section, block)
+            hand_over(k, diagonal, block)
+
+        @pl.when((section != helper) & (section != diagonal))
+        def _():
+            wait_for(column_part(k, 1), grad_recv.at[2, k])
+
+            @pl.when(section != block)
+            def _():
+                hand_over(k, section, block)
+
+    def to_sections_all(k):
+        sum_cores(k)
+        section_part[k, 0, section] = own_part[k, :, tile(section)]
+        for step in range(1, sections):
+            other = lax.rem(section + step, sections)
+            send_tile(k, other, 0, other)
+
+    def to_column_all(k):
+        wait_for(section_part.at[k, 0, pl.ds(0, sections - 1)], grad_recv.at[1, k])
+        reduce_tile(k, 0, section)
 
     def to_all(k):
-        column_arrived(k)
-        place = whole.at[k, :, :, core, rows16]
+        wait_for(column_part(k, 1), grad_recv.at[2, k])
+        place = whole.at[k, :, :, core, tile(section)]
         for step in range(1, sections):
             other = lax.rem(section + step, sections)
             remote(place, place, grad_send.at[3, k], grad_recv.at[3, k], at(other_section=other)).start()
@@ -521,9 +587,6 @@
 
     def shared(k):
         wait_for(whole.at[k, :, :, 0], grad_recv.at[4, k])
-
-    def block_of(k):
-        return lax.div(k - 1, 2)
 
     def when_due(k, act):
         @pl.when(k <= stages - 1)
@@ -583,7 +646,7 @@
                 shifted.at[number], lambda tap: weights[2 * s + 1, channels * tap : channels * (tap + 1), :], channels
             )
         when_due(stage + 2, to_sections)
-        when_due(stage + 6, to_owner)
+        when_due(stage + 5, to_owner)
         backward_stage(stage, vector(0), vector(1), lambda number: held[number], during_first)
         for number in range(chips):
             passed = conv_transposed(
@@ -591,7 +654,7 @@
             )
             upstream[number] = (upstream[number].astype(f32) + passed).astype(bf16)
         when_due(stage + 1, to_sections)
-        when_due(stage + 5, to_owner)
+        when_due(stage + 4, to_owner)
         return 0
 
     lax.fori_loop(0, blocks, block_back, 0)
@@ -628,9 +691,8 @@
     remote(
         flat.at[sent_rows], flat_core, grad_send.at[0, extra], grad_recv.at[0, extra], at(other=sibling)
     ).start()
-    to_sections(0)
+    to_sections_all(0)
     to_column(2)
-    to_owner(5)
     for step in range(1, sections):
         remote(
             totals.at[section], totals.at[section], total_send, total_recv,
@@ -675,11 +737,11 @@
     lax.fori_loop(0, bins, store_bin, 0)
 
     to_owner(3)
-    to_column(0)
+    to_column_all(0)
     wait_for(flat_section.at[pl.ds(0, sections - 1)], grad_recv.at[1, extra])
     piece = total_of(flat_section[number].astype(f32) for number in range(sections)).astype(bf16)
     flat_place = flat_whole.at[row_half, core, flat48, lanes]
-    flat_place[...] = over_groups(0, piece, flat_group, extra)
+    flat_place[...] = over_groups(0, 0, piece, flat_group, extra)
     for step in range(1, chips):
         remote(
             flat_place, flat_place, grad_send.at[2, extra], grad_recv.at[2, extra], at(other=chip_peer(step))
@@ -755,22 +817,50 @@
     lax.fori_loop(0, 2 * blocks, drain_weights, 0)
 
     def drain_grads(k, unused):
+        block, diagonal, helper = roles(k)
+        own_tiles = section_part.at[k, 0]
+        column = whole.at[k, :, :, 0]
         wait_for(core_part.at[k], grad_send.at[0, k])
-        wait_for(section_part.at[k, pl.ds(0, sections - 1)], grad_send.at[1, k])
-        wait_for(whole.at[k, :, 0, 0, pl.ds(0, 16 * (chips - 1)), pl.ds(0, half)], grad_send.at[2, k])
+
+        @pl.when(section == diagonal)
+        def _():
+            wait_for(own_tiles.at[pl.ds(0, 4)], grad_send.at[1, k])
+
+        @pl.when(section == helper)
+        def _():
+            wait_for(own_tiles.at[pl.ds(0, 2)], grad_send.at[1, k])
+            wait_for(column_part(k, 2), grad_send.at[2, k])
+            wait_for(column.at[:, :, pl.ds(0, 32)], grad_send.at[3, k])
+
+        @pl.when((section != helper) & (section != diagonal))
+        def _():
+            wait_for(own_tiles.at[pl.ds(0, 3)], grad_send.at[1, k])
+            wait_for(column_part(k, 1), grad_send.at[2, k])
+
+            @pl.when(section != block)
+            def _():
+                wait_for(column.at[:, :, pl.ds(0, 16)], grad_send.at[3, k])
+
+        @pl.when(section == block)
+        def _():
+            wait_for(column, grad_send.at[4, k])
+
         if groups > 1:
-            wait_for(group_part.at[k, pl.ds(0, groups - 1)], group_send.at[k])
-
-        @pl.when((k > 0) & (section != block_of(k)))
-        def _():
-            wait_for(whole.at[k, :, :, 0, pl.ds(0, 16)], grad_send.at[3, k])
-
-        @pl.when((k > 0) & (section == block_of(k)))
-        def _():
-            wait_for(whole.at[k, :, :, 0], grad_send.at[4, k])
+            @pl.when(section != diagonal)
+            def _():
+                wait_for(group_part.at[k, 0, pl.ds(0, groups - 1)], group_send.at[0, k])
+
+            @pl.when(section == helper)
+            def _():
+                wait_for(group_part.at[k, 1, pl.ds(0, groups - 1)], group_send.at[1, k])
         return 0
 
-    lax.fori_loop(0, stages, drain_grads, 0)
+    lax.fori_loop(1, stages, drain_grads, 0)
+    wait_for(core_part.at[0], grad_send.at[0, 0])
+    wait_for(section_part.at[0, 0, pl.ds(0, sections - 1)], grad_send.at[1, 0])
+    wait_for(column_part(0, 1), grad_send.at[2, 0])
+    if groups > 1:
+        wait_for(group_part.at[0, 0, pl.ds(0, groups - 1)], group_send.at[0, 0])
     wait_for(whole.at[0, :, :, 0, pl.ds(0, 16 * (sections - 1))], grad_send.at[3, 0])
     wait_for(whole.at[0, :, :, 0], grad_send.at[4, 0])
     wait_for(flat_core, grad_send.at[0, extra])
@@ -779,7 +869,7 @@
     wait_for(flat_whole.at[:, 0, pl.ds(0, 48 * (sections - 1))], grad_send.at[3, extra])
     wait_for(flat_whole.at[:, 0], grad_send.at[4, extra])
     if groups > 1:
-        wait_for(flat_group.at[0, pl.ds(0, groups - 1)], group_send.at[extra])
+        wait_for(flat_group.at[0, 0, pl.ds(0, groups - 1)], group_send.at[0, extra])
     first_copy.wait()
     second_copy.wait()
     unite_done.wait()
@@ -892,7 +982,7 @@
             pltpu.VMEM((stages, 9, 2, 64, half), bf16),
             pltpu.VMEM((stages, 9, 64, half), bf16),
             pltpu.VMEM((stages, 9, 64, half), bf16),
-            pltpu.VMEM((stages, sections, 9, 16, half), bf16),
+            pltpu.VMEM((stages, 2, sections, 9, 16, half), bf16),
             pltpu.VMEM((stages, 9, 2, 2, 64, channels), bf16),
             pltpu.VMEM((flat_rows, half), bf16),
             pltpu.VMEM((flat_rows // 4, half), bf16),
@@ -900,15 +990,15 @@
             pltpu.VMEM((sections, 48, half), bf16),
             pltpu.VMEM((2, 2, flat_rows // 4, channels), bf16),
             pltpu.VMEM((sections, stages, 2, channels), f32),
-            pltpu.VMEM((stages if groups > 1 else 1, groups, 9, 16, half), bf16),
-            pltpu.VMEM((1, groups, 48, half), bf16),
+            pltpu.VMEM((stages if groups > 1 else 1, 2, groups, 9, 16, half), bf16),
+            pltpu.VMEM((1, 1, groups, 48, half), bf16),
             dma((9,)), dma, dma, dma((events,)), dma((events,)), dma((chips,)), dma((chips,)), dma((chips,)),
             dma((chips,)), dma((chips,)), dma((chips,)), dma((chips,)), dma((chips,)), dma((4,)),
             dma((2 * blocks,)), dma((2,)), dma((2 * blocks,)), dma((2 * blocks,)), dma, dma,
-            dma((5, stages + 1)), dma((5, stages + 1)), dma, dma, dma((stages + 1,)), dma((stages + 1,)),
+            dma((5, stages + 1)), dma((5, stages + 1)), dma, dma, dma((2, stages + 1)), dma((2, stages + 1)),
         ],
         compiler_params=pltpu.CompilerParams(
-            collective_id=0, has_side_effects=True, vmem_limit_bytes=56 << 20
+            collective_id=0, has_side_effects=True, vmem_limit_bytes=60 << 20
         ),
     )(
         lidar.reshape(cells, channels), context.reshape(pixels, cam).T, depth_logits.reshape(pixels, bins).T,

time: 149 us -> 141 us (0.946); the launches traced: 149 us -> 138 us
  Pallas kernels: 148 us -> 137 us
    pallas_call x1, Pallas kernels: 143 us -> 132 us  [body(): pl.pallas_call(functools.partial(kernel, peers, sections), out_shape=(sha...]
where the time goes in v4:
time: 141 us; the launch traced here: 138 us
  Pallas kernels  137 us (97%)
    pallas_call x1, Pallas kernels, body(): pl.pallas_call(functools.partial(kernel, peers, sections), out_shape=(sha...  132 us
    pallas_call x1, Pallas kernels, body(): pl.pallas_call(functools.partial(widen, cam), out_shape=(shape((cells, ch...  5.06 us

profile of v4, /device:TPU:0, one launch (start us, length us, event | category | flops | bytes accessed | tf_op | source)
XLA Modules:
  0.0 138.0 jit_solution(7256000014423773630)
XLA Ops:
  0.7 132.1 %shard_map.237 = (f32[256,256]{1,0:T(8,128)}, f32[256,256]{1,0:T(8,128)}, f32[80,128]{1,0:T(8,128)}, f32[118,1,128]{2,1,0:T(1,128)}, bf16[9,2,2,64,256]{4,3,2,1,...) custom-call(bf16[256,256]{1,0:T(8,128)(2,1)} %bitcast.40, ...), custom_call_target="tpu_custom_call" | custom-call | tf_op jit(solution)/shard_map/pallas_call | solution.py:945
  132.8 5.1 %shard_map.238 = (f32[256,256]{1,0:T(8,128)}, f32[256,256]{1,0:T(8,128)}, f32[80,128]{1,0:T(8,128)}, f32[118,1,128]{2,1,0:T(1,128)}, f32[1,256]{1,0:T(1,128)}, /...) custom-call(bf16[9,256,256]{2,1,0:T(8,128)(2,1)} %bitcast.35, ...), custom_call_target="tpu_custom_call" | custom-call | tf_op jit(solution)/shard_map/pallas_call | solution.py:1011

commit v5 on v4

--- a/solution.py
+++ b/solution.py
@@ -15,6 +15,8 @@
 wide = 384
 chips = 4
 half = 128
+column_lag = 4
+owner_lag = 8
 flat_rows = 768
 transposed_rhs = (((1,), (1,)), ((), ()))
 transposed_lhs = (((0,), (0,)), ((), ()))
@@ -95,7 +97,7 @@
     weights, unite_weight, vectors, joined, shifted, current, kept, normed, scales, held, gathered, upstream,
     lidars, cameras, mine, slots, unite_mine, unite_slots, probability, places, histogram,
     partial, core_part, own_part, section_part, whole, flat, flat_core, flat_own, flat_section, flat_whole,
-    totals, group_part, flat_group,
+    totals, gains, group_part, flat_group,
     local_sem, unite_send, unite_recv, stat_send, stat_recv, raw_send, raw_recv, cot_send, cot_recv,
     lidar_send, lidar_recv, camera_send, camera_recv, weight_send, weight_recv, relay_send, pass_send, pass_recv,
     vector_send, vector_recv, grad_send, grad_recv, total_send, total_recv, group_send, group_recv,
@@ -365,66 +367,69 @@
         wait_for(slots.at[event, pl.ds(0, members - 1)], stat_recv.at[event])
         return slots[event, :, 0, :], slots[event, :, 1, :]
 
-    def forward_stage(stage, weight, meanwhile, use):
-        centers, squares = [], []
-        for number in range(chips):
-            activ = conv(shifted.at[number], weight)
-            held[number] = activ
-            center = jnp.sum(activ, axis=0, keepdims=True) * (1.0 / cells)
-            offsets = activ - center
-            centers.append(center)
-            squares.append(jnp.sum(offsets * offsets, axis=0, keepdims=True))
-        center, square = merged(jnp.concatenate(centers, axis=0), jnp.concatenate(squares, axis=0), cells)
-        send_stats(stage - 1, center, square)
-        meanwhile()
+    def local_sums(parts):
+        centers, squares = zip(*parts)
+        return merged(jnp.concatenate(centers, axis=0), jnp.concatenate(squares, axis=0), cells)
+
+    def start_conv(number, index):
+        activ = conv(shifted.at[number], lambda i: weights[index, 3 * channels * i : 3 * channels * (i + 1), :])
+        held[number] = activ
+        center = jnp.sum(activ, axis=0, keepdims=True) * (1.0 / cells)
+        offsets = activ - center
+        return center, jnp.sum(offsets * offsets, axis=0, keepdims=True)
+
+    def whole_sums(stage):
         centers, squares = take_stats(stage - 1)
         center, square = merged(centers, squares, chips * cells)
         scale = lax.rsqrt(square * (1.0 / count) + eps)
         scales[stage] = scale
+        return center, scale
+
+    def block(s, last):
+        stage = 2 * s + 1
+
+        def vector(number):
+            return vectors[s, number : number + 1]
+
+        point("first", s)
+        ready(s, 1)
+        center, scale = whole_sums(stage)
+        parts = []
         for number in range(chips):
             value = (held[number] - center) * scale
             normed[stage, number] = value
-            use(number, value)
-
-    def block(s, unused):
-        stage = 2 * s + 1
-
-        def vector(number):
-            return vectors[s, number : number + 1]
-
-        def during_first():
-            point("first", s)
-
-        def during_second():
-            point("second", s)
-
-        def use_first(number, value):
             hidden = silu(vector(0) * value + vector(1))
             kept[stage, number] = hidden.astype(bf16)
             put_shifted(shifted.at[number], hidden, channels)
-
-        def use_second(number, value):
+            parts.append(start_conv(number, 2 * s + 1))
+        send_stats(stage, *local_sums(parts))
+        point("second", s)
+        if not last:
+            ready(s + 1, 0)
+        center, scale = whole_sums(stage + 1)
+        parts = []
+        for number in range(chips):
+            value = (held[number] - center) * scale
+            normed[stage + 1, number] = value
             output = current[number].astype(f32) + silu(vector(2) * value + vector(3))
-            held[number] = output
-            current[number] = output.astype(bf16)
-
-            @pl.when(s < blocks - 1)
-            def _():
+            if last:
+                held[number] = output
+            else:
+                current[number] = output.astype(bf16)
                 kept[stage + 1, number] = output.astype(bf16)
                 put_shifted(shifted.at[number], output, channels)
-
-        ready(s, 0)
-        forward_stage(
-            stage, lambda i: weights[2 * s, 3 * channels * i : 3 * channels * (i + 1), :], during_first, use_first
-        )
-        ready(s, 1)
-        forward_stage(
-            stage + 1, lambda i: weights[2 * s + 1, 3 * channels * i : 3 * channels * (i + 1), :],
-            during_second, use_second,
-        )
+                parts.append(start_conv(number, 2 * s + 2))
+        if not last:
+            send_stats(stage + 1, *local_sums(parts))
+
+    def block_step(s, unused):
+        block(s, False)
         return 0
 
-    lax.fori_loop(0, blocks, block, 0)
+    ready(0, 0)
+    send_stats(0, *local_sums([start_conv(number, 0) for number in range(chips)]))
+    lax.fori_loop(0, blocks - 1, block_step, 0)
+    block(blocks - 1, True)
     act_ref[...] = held[chip]
 
     lanes = pl.ds(pl.multiple_of(lane_half * half, half), half)
@@ -588,40 +593,75 @@
     def shared(k):
         wait_for(whole.at[k, :, :, 0], grad_recv.at[4, k])
 
+    def backwards(first, last, act):
+        def step(number, unused):
+            act(first - number)
+            return 0
+
+        lax.fori_loop(0, first - last + 1, step, 0)
+
     def when_due(k, act):
         @pl.when(k <= stages - 1)
         def _():
             act(k)
 
-    def backward_stage(stage, gain, bias, gradient, meanwhile):
-        event = stages - 1 + stage
-        firsts, seconds = None, None
-        for number in range(chips):
-            value = normed[stage, number]
-            grads = gradient(number) * slope(gain * value + bias)
-            held[number] = grads
-            first = jnp.sum(grads, axis=0, keepdims=True)
-            second = jnp.sum(grads * value, axis=0, keepdims=True)
-            firsts = first if firsts is None else firsts + first
-            seconds = second if seconds is None else seconds + second
-        send_stats(event, firsts, seconds)
-        meanwhile()
-        first, second = take_stats(event)
+    def start_norm(stage, number, grads, gain, bias):
+        value = normed[stage, number]
+        grads = grads * slope(gain * value + bias)
+        held[number] = grads
+        return jnp.sum(grads, axis=0, keepdims=True), jnp.sum(grads * value, axis=0, keepdims=True)
+
+    def send_sums(stage, parts):
+        firsts, seconds = zip(*parts)
+        send_stats(stages - 1 + stage, total_of(firsts), total_of(seconds))
+
+    def norm_factors(stage, gain):
+        first, second = take_stats(stages - 1 + stage)
         first = jnp.sum(first, axis=0, keepdims=True)
         second = jnp.sum(second, axis=0, keepdims=True)
         totals[section, stage, 0:1] = first
         totals[section, stage, 1:2] = second
-        first = first * (1.0 / count)
-        second = second * (1.0 / count)
-        factor = gain * scales[stage]
-        for number in range(chips):
-            put_shifted(
-                shifted.at[number], factor * (held[number] - first - normed[stage, number] * second), channels
-            )
+        return gain * scales[stage], first * (1.0 / count), second * (1.0 / count)
+
+    def end_norm(stage, number, factors):
+        factor, first, second = factors
+        put_shifted(
+            shifted.at[number], factor * (held[number] - first - normed[stage, number] * second), channels
+        )
+
+    def passed(number, index):
+        return conv_transposed(
+            shifted.at[number], lambda tap: weights[index, channels * tap : channels * (tap + 1), :], channels
+        )
+
+    def during(stage):
+        weight_grad(stage + 1, kept.at[stage])
+        when_due(stage + 2, to_sections)
+        when_due(stage + column_lag, to_column)
+        when_due(stage + owner_lag, to_owner)
 
     for step in range(1, chips):
         wait_for(upstream.at[0], cot_recv.at[step])
         wait_for(upstream.at[0], cot_send.at[step])
+    def take_gains(s):
+        @pl.when(s > 0)
+        def _():
+            gains[0:1] = vectors[jnp.maximum(s - 1, 0), 2:3]
+            gains[1:2] = vectors[jnp.maximum(s - 1, 0), 3:4]
+
+        @pl.when(s == 0)
+        def _():
+            gains[0:1] = unite_gain[...]
+            gains[1:2] = unite_bias[...]
+
+    take_gains(blocks)
+    send_sums(
+        stages - 1,
+        [
+            start_norm(stages - 1, number, upstream[number].astype(f32), gains[0:1], gains[1:2])
+            for number in range(chips)
+        ],
+    )
 
     def block_back(back, unused):
         s = blocks - 1 - back
@@ -630,45 +670,37 @@
         def vector(number):
             return vectors[s, number : number + 1]
 
-        def during_second():
-            @pl.when(back > 0)
-            def _():
-                weight_grad(stage + 2, kept.at[stage + 1])
-            when_due(stage + 4, to_column)
-
-        def during_first():
-            weight_grad(stage + 1, kept.at[stage])
-            when_due(stage + 3, to_column)
-
-        backward_stage(stage + 1, vector(2), vector(3), lambda number: upstream[number].astype(f32), during_second)
+        @pl.when(back > 0)
+        def _():
+            during(stage + 1)
+
+        factors = norm_factors(stage + 1, vector(2))
+        parts = []
         for number in range(chips):
-            held[number] = conv_transposed(
-                shifted.at[number], lambda tap: weights[2 * s + 1, channels * tap : channels * (tap + 1), :], channels
-            )
-        when_due(stage + 2, to_sections)
-        when_due(stage + 5, to_owner)
-        backward_stage(stage, vector(0), vector(1), lambda number: held[number], during_first)
+            end_norm(stage + 1, number, factors)
+            parts.append(start_norm(stage, number, passed(number, 2 * s + 1), vector(0), vector(1)))
+        send_sums(stage, parts)
+        during(stage)
+        take_gains(s)
+        factors = norm_factors(stage, vector(0))
+        parts = []
         for number in range(chips):
-            passed = conv_transposed(
-                shifted.at[number], lambda tap: weights[2 * s, channels * tap : channels * (tap + 1), :], channels
-            )
-            upstream[number] = (upstream[number].astype(f32) + passed).astype(bf16)
-        when_due(stage + 1, to_sections)
-        when_due(stage + 4, to_owner)
+            end_norm(stage, number, factors)
+            grads = (upstream[number].astype(f32) + passed(number, 2 * s)).astype(bf16)
+            upstream[number] = grads
+            parts.append(start_norm(stage - 1, number, grads.astype(f32), gains[0:1], gains[1:2]))
+        send_sums(stage - 1, parts)
         return 0
 
     lax.fori_loop(0, blocks, block_back, 0)
 
-    def during_unite():
-        weight_grad(1, kept.at[0])
-        to_column(3)
-
-    backward_stage(
-        0, unite_gain[...], unite_bias[...], lambda number: upstream[number].astype(f32), during_unite
-    )
+    during(0)
     for step in range(1, chips):
         wait_for(lidars.at[0], lidar_recv.at[step])
         wait_for(cameras.at[0], camera_recv.at[step])
+    factors = norm_factors(0, gains[0:1])
+    for number in range(chips):
+        end_norm(0, number, factors)
     weight_grad(0, lidars)
     to_sections(1)
     held_cameras = [cameras[number] for number in range(chips)]
@@ -692,7 +724,7 @@
         flat.at[sent_rows], flat_core, grad_send.at[0, extra], grad_recv.at[0, extra], at(other=sibling)
     ).start()
     to_sections_all(0)
-    to_column(2)
+    backwards(min(column_lag - 1, stages - 1), 2, to_column)
     for step in range(1, sections):
         remote(
             totals.at[section], totals.at[section], total_send, total_recv,
@@ -712,7 +744,6 @@
             flat_own.at[pl.ds(pl.multiple_of(other * 48, 16), 48)], flat_section.at[section],
             grad_send.at[1, extra], grad_recv.at[1, extra], at(other_section=other),
         ).start()
-    to_owner(4)
     lidar_grad[...] = conv_transposed(
         own, lambda tap: unite_weight[united_in * tap : united_in * tap + channels, :], channels
     )
@@ -736,7 +767,6 @@
 
     lax.fori_loop(0, bins, store_bin, 0)
 
-    to_owner(3)
     to_column_all(0)
     wait_for(flat_section.at[pl.ds(0, sections - 1)], grad_recv.at[1, extra])
     piece = total_of(flat_section[number].astype(f32) for number in range(sections)).astype(bf16)
@@ -746,8 +776,7 @@
         remote(
             flat_place, flat_place, grad_send.at[2, extra], grad_recv.at[2, extra], at(other=chip_peer(step))
         ).start()
-    to_owner(2)
-    to_owner(1)
+    backwards(min(owner_lag - 1, stages - 1), 1, to_owner)
     to_all(0)
     wait_for(flat_whole.at[0, 0, pl.ds(0, 48 * (chips - 1)), pl.ds(0, half)], grad_recv.at[2, extra])
     flat_rows_place = flat_whole.at[:, core, flat48]
@@ -758,11 +787,7 @@
             at(other_section=other),
         ).start()
 
-    def share_all(back, unused):
-        owner_share(stages - 1 - back)
-        return 0
-
-    lax.fori_loop(0, stages - 1, share_all, 0)
+    backwards(stages - 1, 1, owner_share)
     share(0)
     wait_for(flat_whole.at[:, 0, pl.ds(0, 48 * (sections - 1))], grad_recv.at[3, extra])
     flat_half = flat_whole.at[:, core]
@@ -990,6 +1015,7 @@
             pltpu.VMEM((sections, 48, half), bf16),
             pltpu.VMEM((2, 2, flat_rows // 4, channels), bf16),
             pltpu.VMEM((sections, stages, 2, channels), f32),
+            pltpu.VMEM((2, channels), f32),
             pltpu.VMEM((stages if groups > 1 else 1, 2, groups, 9, 16, half), bf16),
             pltpu.VMEM((1, 1, groups, 48, half), bf16),
             dma((9,)), dma, dma, dma((events,)), dma((events,)), dma((chips,)), dma((chips,)), dma((chips,)),

time: 141 us -> 133 us (0.943); the launches traced: 138 us -> 133 us
  Pallas kernels: 137 us -> 132 us
    pallas_call x1, Pallas kernels: 132 us -> 127 us  [body(): pl.pallas_call(functools.partial(kernel, peers, sections), out_shape=(sha...]
where the time goes in v5:
time: 133 us
  Pallas kernels  132 us (99%)
    pallas_call x1, Pallas kernels, body(): pl.pallas_call(functools.partial(kernel, peers, sections), out_shape=(sha...  127 us
    pallas_call x1, Pallas kernels, body(): pl.pallas_call(functools.partial(widen, cam), out_shape=(shape((cells, ch...  5.06 us

profile of v5, /device:TPU:0, one launch (start us, length us, event | category | flops | bytes accessed | tf_op | source)
XLA Modules:
  0.0 132.8 jit_solution(12231375590662448946)
XLA Ops:
  0.7 126.9 %shard_map.237 = (f32[256,256]{1,0:T(8,128)}, f32[256,256]{1,0:T(8,128)}, f32[80,128]{1,0:T(8,128)}, f32[118,1,128]{2,1,0:T(1,128)}, bf16[9,2,2,64,256]{4,3,2,1,...) custom-call(bf16[256,256]{1,0:T(8,128)(2,1)} %bitcast.40, ...), custom_call_target="tpu_custom_call" | custom-call | tf_op jit(solution)/shard_map/pallas_call | solution.py:970
  127.6 5.1 %shard_map.238 = (f32[256,256]{1,0:T(8,128)}, f32[256,256]{1,0:T(8,128)}, f32[80,128]{1,0:T(8,128)}, f32[118,1,128]{2,1,0:T(1,128)}, f32[1,256]{1,0:T(1,128)}, /...) custom-call(bf16[9,256,256]{2,1,0:T(8,128)(2,1)} %bitcast.35, ...), custom_call_target="tpu_custom_call" | custom-call | tf_op jit(solution)/shard_map/pallas_call | solution.py:1037

commit v6 on v5

--- a/solution.py
+++ b/solution.py
@@ -22,27 +22,26 @@
 transposed_lhs = (((0,), (0,)), ((), ()))
 
 
-def sigmoid(value):
-    return 0.5 * jnp.tanh(0.5 * value) + 0.5
-
-
-def slope(value):
-    gate = sigmoid(value)
-    return gate * (1.0 + value * (1.0 - gate))
-
-
-def silu(value):
-    return value * sigmoid(value)
+def silu_of_half(half_value):
+    return half_value + half_value * jnp.tanh(half_value)
+
+
+def twice_slope_of_half(half_value):
+    bent = jnp.tanh(half_value)
+    return 1.0 + bent + half_value * (1.0 - bent * bent)
 
 
 def put_shifted(buffer, value, stride, offset=0):
-    column = lax.broadcasted_iota(jnp.int32, (cells, 1), 0) % side
     width = value.shape[1]
-    before = jnp.where(column == 0, 0.0, pltpu.roll(value, 1, 0))
-    after = jnp.where(column == side - 1, 0.0, pltpu.roll(value, cells - 1, 0))
-    for group, shifted in enumerate((before, value, after)):
+    split = value.reshape(side, 2, 8, width)
+    row = lax.broadcasted_iota(jnp.int32, (1, 8, width), 1)
+    down = pltpu.roll(split, 1, 2)
+    up = pltpu.roll(split, 7, 2)
+    before = jnp.stack([jnp.where(row == 0, 0.0, down[:, 0]), jnp.where(row == 0, down[:, 0], down[:, 1])], axis=1)
+    after = jnp.stack([jnp.where(row == 7, up[:, 1], up[:, 0]), jnp.where(row == 7, 0.0, up[:, 1])], axis=1)
+    for group, shifted in enumerate((before, split, after)):
         start = group * stride + offset
-        buffer[side : side + cells, start : start + width] = shifted.astype(bf16)
+        buffer[side : side + cells, start : start + width] = shifted.reshape(cells, width).astype(bf16)
 
 
 def total_of(terms):
@@ -94,7 +93,7 @@
     lidar_ref, context_ref, logit_ref, cell_ref, unite_ref, unite_gain, unite_bias, first_ref, second_ref,
     first_gain, first_bias, second_gain, second_bias, cotangent_ref,
     act_ref, lidar_grad, context_grad, logit_grad, unite_out, camera_out, first_out, second_out, small_out,
-    weights, unite_weight, vectors, joined, shifted, current, kept, normed, scales, held, gathered, upstream,
+    weights, unite_weight, vectors, joined, shifted, current, kept, halves, scales, held, gathered, upstream,
     lidars, cameras, mine, slots, unite_mine, unite_slots, probability, places, histogram,
     partial, core_part, own_part, section_part, whole, flat, flat_core, flat_own, flat_section, flat_whole,
     totals, gains, group_part, flat_group,
@@ -320,10 +319,16 @@
     scales[stages] = center
     point("merged")
 
+    def half_affine(center, scale, gain, bias):
+        factor = 0.5 * gain * scale
+        return factor, 0.5 * bias - center * factor
+
+    factor, offset = half_affine(scales[stages], scales[0], unite_gain[...], unite_bias[...])
+
     def enter(number):
-        value = (gathered[number].astype(f32) - scales[stages]) * scales[0]
-        normed[0, number] = value
-        entering = silu(unite_gain[...] * value + unite_bias[...])
+        value = gathered[number].astype(f32) * factor + offset
+        halves[0, number] = value
+        entering = silu_of_half(value)
         current[number] = entering.astype(bf16)
         kept[0, number] = entering.astype(bf16)
         put_shifted(shifted.at[number], entering, channels)
@@ -393,12 +398,12 @@
 
         point("first", s)
         ready(s, 1)
-        center, scale = whole_sums(stage)
+        factor, offset = half_affine(*whole_sums(stage), vector(0), vector(1))
         parts = []
         for number in range(chips):
-            value = (held[number] - center) * scale
-            normed[stage, number] = value
-            hidden = silu(vector(0) * value + vector(1))
+            value = held[number] * factor + offset
+            halves[stage, number] = value
+            hidden = silu_of_half(value)
             kept[stage, number] = hidden.astype(bf16)
             put_shifted(shifted.at[number], hidden, channels)
             parts.append(start_conv(number, 2 * s + 1))
@@ -406,12 +411,12 @@
         point("second", s)
         if not last:
             ready(s + 1, 0)
-        center, scale = whole_sums(stage + 1)
+        factor, offset = half_affine(*whole_sums(stage + 1), vector(2), vector(3))
         parts = []
         for number in range(chips):
-            value = (held[number] - center) * scale
-            normed[stage + 1, number] = value
-            output = current[number].astype(f32) + silu(vector(2) * value + vector(3))
+            value = held[number] * factor + offset
+            halves[stage + 1, number] = value
+            output = current[number].astype(f32) + silu_of_half(value)
             if last:
                 held[number] = output
             else:
@@ -605,28 +610,32 @@
         def _():
             act(k)
 
-    def start_norm(stage, number, grads, gain, bias):
-        value = normed[stage, number]
-        grads = grads * slope(gain * value + bias)
+    def start_norm(stage, number, grads):
+        value = halves[stage, number]
+        grads = grads * twice_slope_of_half(value)
         held[number] = grads
         return jnp.sum(grads, axis=0, keepdims=True), jnp.sum(grads * value, axis=0, keepdims=True)
 
-    def send_sums(stage, parts):
+    def send_sums(stage, parts, gain, bias):
         firsts, seconds = zip(*parts)
-        send_stats(stages - 1 + stage, total_of(firsts), total_of(seconds))
-
-    def norm_factors(stage, gain):
+        first = 0.5 * total_of(firsts)
+        send_stats(stages - 1 + stage, first, (total_of(seconds) - bias * first) / gain)
+
+    def norm_factors(stage, gain, bias):
         first, second = take_stats(stages - 1 + stage)
         first = jnp.sum(first, axis=0, keepdims=True)
         second = jnp.sum(second, axis=0, keepdims=True)
         totals[section, stage, 0:1] = first
         totals[section, stage, 1:2] = second
-        return gain * scales[stage], first * (1.0 / count), second * (1.0 / count)
+        first = first * (1.0 / count)
+        second = second * (1.0 / count)
+        scale = scales[stage]
+        return 0.5 * gain * scale, 2.0 * scale * second, scale * (gain * first - bias * second)
 
     def end_norm(stage, number, factors):
-        factor, first, second = factors
+        by_grads, by_halves, constant = factors
         put_shifted(
-            shifted.at[number], factor * (held[number] - first - normed[stage, number] * second), channels
+            shifted.at[number], held[number] * by_grads - halves[stage, number] * by_halves - constant, channels
         )
 
     def passed(number, index):
@@ -635,8 +644,8 @@
         )
 
     def during(stage):
+        when_due(stage + 2, to_sections)
         weight_grad(stage + 1, kept.at[stage])
-        when_due(stage + 2, to_sections)
         when_due(stage + column_lag, to_column)
         when_due(stage + owner_lag, to_owner)
 
@@ -658,9 +667,10 @@
     send_sums(
         stages - 1,
         [
-            start_norm(stages - 1, number, upstream[number].astype(f32), gains[0:1], gains[1:2])
+            start_norm(stages - 1, number, upstream[number].astype(f32))
             for number in range(chips)
         ],
+        gains[0:1], gains[1:2],
     )
 
     def block_back(back, unused):
@@ -674,22 +684,22 @@
         def _():
             during(stage + 1)
 
-        factors = norm_factors(stage + 1, vector(2))
+        factors = norm_factors(stage + 1, vector(2), vector(3))
         parts = []
         for number in range(chips):
             end_norm(stage + 1, number, factors)
-            parts.append(start_norm(stage, number, passed(number, 2 * s + 1), vector(0), vector(1)))
-        send_sums(stage, parts)
+            parts.append(start_norm(stage, number, passed(number, 2 * s + 1)))
+        send_sums(stage, parts, vector(0), vector(1))
         during(stage)
         take_gains(s)
-        factors = norm_factors(stage, vector(0))
+        factors = norm_factors(stage, vector(0), vector(1))
         parts = []
         for number in range(chips):
             end_norm(stage, number, factors)
             grads = (upstream[number].astype(f32) + passed(number, 2 * s)).astype(bf16)
             upstream[number] = grads
-            parts.append(start_norm(stage - 1, number, grads.astype(f32), gains[0:1], gains[1:2]))
-        send_sums(stage - 1, parts)
+            parts.append(start_norm(stage - 1, number, grads.astype(f32)))
+        send_sums(stage - 1, parts, gains[0:1], gains[1:2])
         return 0
 
     lax.fori_loop(0, blocks, block_back, 0)
@@ -698,7 +708,7 @@
     for step in range(1, chips):
         wait_for(lidars.at[0], lidar_recv.at[step])
         wait_for(cameras.at[0], camera_recv.at[step])
-    factors = norm_factors(0, gains[0:1])
+    factors = norm_factors(0, unite_gain[...], unite_bias[...])
     for number in range(chips):
         end_norm(0, number, factors)
     weight_grad(0, lidars)

time: 133 us -> 132 us (level)
    pallas_call x1, Pallas kernels: 127 us -> 126 us  [body(): pl.pallas_call(functools.partial(kernel, peers, sections), out_shape=(sha...]
where the time goes in v6:
time: 132 us; the launch traced here: 131 us
  Pallas kernels  131 us (99%)
    pallas_call x1, Pallas kernels, body(): pl.pallas_call(functools.partial(kernel, peers, sections), out_shape=(sha...  126 us
    pallas_call x1, Pallas kernels, body(): pl.pallas_call(functools.partial(widen, cam), out_shape=(shape((cells, ch...  5.06 us

profile of v6, /device:TPU:0, one launch (start us, length us, event | category | flops | bytes accessed | tf_op | source)
XLA Modules:
  0.0 131.4 jit_solution(3657067376685169634)
XLA Ops:
  0.7 125.6 %shard_map.237 = (f32[256,256]{1,0:T(8,128)}, f32[256,256]{1,0:T(8,128)}, f32[80,128]{1,0:T(8,128)}, f32[118,1,128]{2,1,0:T(1,128)}, bf16[9,2,2,64,256]{4,3,2,1,...) custom-call(bf16[256,256]{1,0:T(8,128)(2,1)} %bitcast.40, ...), custom_call_target="tpu_custom_call" | custom-call | tf_op jit(solution)/shard_map/pallas_call | solution.py:980
  126.2 5.1 %shard_map.238 = (f32[256,256]{1,0:T(8,128)}, f32[256,256]{1,0:T(8,128)}, f32[80,128]{1,0:T(8,128)}, f32[118,1,128]{2,1,0:T(1,128)}, f32[1,256]{1,0:T(1,128)}, /...) custom-call(bf16[9,256,256]{2,1,0:T(8,128)(2,1)} %bitcast.35, ...), custom_call_target="tpu_custom_call" | custom-call | tf_op jit(solution)/shard_map/pallas_call | solution.py:1047

commit v7 on v6

--- a/solution.py
+++ b/solution.py
@@ -15,7 +15,7 @@
 wide = 384
 chips = 4
 half = 128
-column_lag = 4
+column_lag = 3
 owner_lag = 8
 flat_rows = 768
 transposed_rhs = (((1,), (1,)), ((), ()))
@@ -71,18 +71,18 @@
 
 
 plan = {
-    "start": [("offer", 0, "near", 0), ("offer", 0, "far", 3), ("offer", 0, "near", 2), ("offer", 0, "near", 1)],
-    "lift2": [("offer", 0, "near", 3), ("offer", 1, "near", 0)],
-    "united": [("relay", 0, 0), ("offer", 1, "near", 1), ("offer", 1, "near", 3)],
-    "united2": [("offer", 1, "far", 0), ("offer", 1, "near", 2), ("offer", 0, "far", 1)],
-    "merged": [("offer", 0, "far", 0), ("relay", 1, 0)],
-    "entered1": [("relay", 3, 0), ("relay", 0, 1), ("relay", 2, 0)],
-    "entered3": [("offer", 0, "far", 2), ("offer", 1, "far", 1)],
-    "entered2": [("relay", 2, 1)],
-    "entered": [("offer", 1, "far", 2), ("arrive", 0, 0)],
-    ("first", 0): [("relay", 1, 1), ("arrive", 1, 0), ("offer", 1, "far", 3), ("arrive", 0, 1)],
+    "start": [("offer", 0, "near", 2), ("offer", 0, "near", 0), ("offer", 0, "near", 1)],
+    "lift1": [("offer", 0, "far", 3), ("offer", 1, "near", 1)],
+    "united": [("offer", 1, "near", 0), ("relay", 0, 0), ("offer", 0, "near", 3)],
+    "united2": [("offer", 1, "near", 2), ("offer", 1, "far", 0)],
+    "merged": [("offer", 0, "far", 0)],
+    "entered1": [("offer", 0, "far", 1)],
+    "entered3": [("relay", 0, 1), ("relay", 1, 0), ("offer", 1, "near", 3)],
+    "entered2": [("relay", 2, 0), ("offer", 1, "far", 1), ("relay", 2, 1)],
+    "entered": [("relay", 3, 0), ("offer", 0, "far", 2), ("arrive", 0, 0)],
+    ("first", 0): [("relay", 1, 1), ("offer", 1, "far", 2), ("offer", 1, "far", 3), ("arrive", 1, 0), ("arrive", 0, 1)],
     ("second", 0): [("relay", 3, 1)],
-    ("first", 1): [("arrive", 1, 1), ("arrive", 2, 0)],
+    ("first", 1): [("arrive", 2, 0), ("arrive", 1, 1)],
     ("second", 1): [("arrive", 3, 0), ("arrive", 2, 1)],
     ("second", 2): [("arrive", 3, 1)],
 }

time: 132 us -> 130 us (0.985)
  Pallas kernels: 131 us -> 128 us
    pallas_call x1, Pallas kernels: 126 us -> 123 us  [body(): pl.pallas_call(functools.partial(kernel, peers, sections), out_shape=(sha...]
where the time goes in v7:
time: 130 us; the launch traced here: 129 us
  Pallas kernels  128 us (98%)
    pallas_call x1, Pallas kernels, body(): pl.pallas_call(functools.partial(kernel, peers, sections), out_shape=(sha...  123 us
    pallas_call x1, Pallas kernels, body(): pl.pallas_call(functools.partial(widen, cam), out_shape=(shape((cells, ch...  5.06 us

profile of v7, /device:TPU:0, one launch (start us, length us, event | category | flops | bytes accessed | tf_op | source)
XLA Modules:
  0.0 128.9 jit_solution(15794492775418918367)
XLA Ops:
  0.7 123.0 %shard_map.237 = (f32[256,256]{1,0:T(8,128)}, f32[256,256]{1,0:T(8,128)}, f32[80,128]{1,0:T(8,128)}, f32[118,1,128]{2,1,0:T(1,128)}, bf16[9,2,2,64,256]{4,3,2,1,...) custom-call(bf16[256,256]{1,0:T(8,128)(2,1)} %bitcast.40, ...), custom_call_target="tpu_custom_call" | custom-call | tf_op jit(solution)/shard_map/pallas_call | solution.py:980
  123.6 5.1 %shard_map.238 = (f32[256,256]{1,0:T(8,128)}, f32[256,256]{1,0:T(8,128)}, f32[80,128]{1,0:T(8,128)}, f32[118,1,128]{2,1,0:T(1,128)}, f32[1,256]{1,0:T(1,128)}, /...) custom-call(bf16[9,256,256]{2,1,0:T(8,128)(2,1)} %bitcast.35, ...), custom_call_target="tpu_custom_call" | custom-call | tf_op jit(solution)/shard_map/pallas_call | solution.py:1047

commit v8 on v7

--- a/solution.py
+++ b/solution.py
@@ -920,8 +920,9 @@
     passed = []
     channels = full[1].shape[-1]
 
-    def store(number, tap):
-        return pltpu.make_async_copy(full[number].at[tap], outs[10 + number].at[tap], out_sem.at[number, tap])
+    def store(number, row):
+        taps = pl.ds(3 * row, 3)
+        return pltpu.make_async_copy(full[number].at[taps], outs[10 + number].at[taps], out_sem.at[number, row])
 
     loads[0].wait()
     loads[1].wait()
@@ -930,19 +931,21 @@
         full[0][tap, 0:channels] = narrow[0][tap].astype(f32)
         rows = pl.ds(pl.multiple_of(cam * tap, 16), cam)
         full[0][tap, channels : channels + cam] = narrow[1][rows].astype(f32)
-        store(0, tap).start()
         return 0
 
-    lax.fori_loop(0, 9, unite_tap, 0)
+    for row in range(3):
+        lax.fori_loop(3 * row, 3 * row + 3, unite_tap, 0)
+        store(0, row).start()
     for number in (1, 2):
         loads[number + 1].wait()
 
         def block_tap(tap, unused):
             full[number][tap] = narrow[number + 1][tap].astype(f32)
-            store(number, tap).start()
             return 0
 
-        lax.fori_loop(0, 9, block_tap, 0)
+        for row in range(3):
+            lax.fori_loop(3 * row, 3 * row + 3, block_tap, 0)
+            store(number, row).start()
     for number in range(4, 9):
         loads[number].wait()
     for number in range(10):
@@ -950,8 +953,8 @@
         passed.append(pltpu.make_async_copy(source, outs[number], plain_sem.at[number]))
         passed[-1].start()
     for number in range(3):
-        for tap in range(9):
-            store(number, tap).wait()
+        for row in range(3):
+            store(number, row).wait()
     for copy in passed:
         copy.wait()
 
@@ -1071,7 +1074,7 @@
             pltpu.VMEM((9, united_in, channels), f32),
             pltpu.VMEM((9, channels, channels), f32),
             pltpu.VMEM((9, channels, channels), f32),
-            dma((9,)), dma((3, 9)), dma((10,)),
+            dma((9,)), dma((3, 3)), dma((10,)),
         ],
         compiler_params=pltpu.CompilerParams(vmem_limit_bytes=60 << 20),
     )(

time: 130 us -> 130 us (level)
  no operation moved by 1% of the time
where the time goes in v8:
time: 130 us; the launch traced here: 129 us
  Pallas kernels  128 us (98%)
    pallas_call x1, Pallas kernels, body(): pl.pallas_call(functools.partial(kernel, peers, sections), out_shape=(sha...  123 us
    pallas_call x1, Pallas kernels, body(): pl.pallas_call(functools.partial(widen, cam), out_shape=(shape((cells, ch...  4.96 us

profile of v8, /device:TPU:0, one launch (start us, length us, event | category | flops | bytes accessed | tf_op | source)
XLA Modules:
  0.0 128.8 jit_solution(2107105270810836572)
XLA Ops:
  0.7 123.0 %shard_map.237 = (f32[256,256]{1,0:T(8,128)}, f32[256,256]{1,0:T(8,128)}, f32[80,128]{1,0:T(8,128)}, f32[118,1,128]{2,1,0:T(1,128)}, bf16[9,2,2,64,256]{4,3,2,1,...) custom-call(bf16[256,256]{1,0:T(8,128)(2,1)} %bitcast.40, ...), custom_call_target="tpu_custom_call" | custom-call | tf_op jit(solution)/shard_map/pallas_call | solution.py:983
  123.6 5.0 %shard_map.238 = (f32[256,256]{1,0:T(8,128)}, f32[256,256]{1,0:T(8,128)}, f32[80,128]{1,0:T(8,128)}, f32[118,1,128]{2,1,0:T(1,128)}, f32[1,256]{1,0:T(1,128)}, /...) custom-call(bf16[9,256,256]{2,1,0:T(8,128)(2,1)} %bitcast.35, ...), custom_call_target="tpu_custom_call" | custom-call | tf_op jit(solution)/shard_map/pallas_call | solution.py:1050
